TPU v7x, 256 devices: a whole 4x4x8 slice. The times are simulated.
256 devices in a mesh: row: 32 (over x, z), feat: 8 (over y, core).
Axes of the slice: x: 4, y: 4, z: 8, core: 2. Of those that a mesh axis runs over, the one named last changes fastest.
Arguments:
- candidates: bfloat16 [2048, 16384], P('row', 'feat'), may hold values from -48 to 48, as said below
- inv_factor: bfloat16 [16384, 16384], P('row', 'feat'), may hold values from -1.5 to 1.5, as said below
- weights: float32 [2048], P('row'), may hold values from 0.01 to 0.1
- strata: int32 [2048], P('row'), may hold values from 0 to 63, never falling along the last dimension, each value on 1 to 256 neighbouring positions
Outputs:
- new_weight: float32 [2048], P('row')
- leverage: float32 [2048], P('row')
- information: float32 [16384, 16384], P('row', 'feat')
Inputs may be any that keep to these rules, and one draw needn't show every extreme that they name: `candidates`: row scales and column scales differ. `inv_factor`: zero above the diagonal, positive on the diagonal.
All inputs are finite; a program needn't handle non-finite values.
Results may differ from a plain program's by a relative error of at most 0.0029.
Values may be sent and summed in bfloat16 or wider, within the bound.
A program may use at most 64 MiB of HBM per device.

v0:
```python
import jax
import jax.numpy as jnp
from jax import lax
from jax.sharding import PartitionSpec as P


def broadcast(shard, axis, root):
    mine = lax.axis_index(axis) == root
    return lax.psum(jnp.where(mine, shard, jnp.zeros_like(shard)), axis)


def per_device(candidates, inv_factor, weights, strata):
    rows_dev = candidates.shape[0]
    feat_block = candidates.shape[1]
    row_block = inv_factor.shape[0]
    row_count = lax.axis_size("row")
    feat_count = lax.axis_size("feat")
    features = feat_block * feat_count
    gathered = lax.all_gather(candidates, "row", axis=0, tiled=True)
    partial_value = lax.dot_general(
        gathered, inv_factor, (((1,), (1,)), ((), ())), preferred_element_type=jnp.float32
    )
    shaped = partial_value.reshape(row_count, rows_dev, row_block)
    summed = lax.psum_scatter(shaped, "feat", scatter_dimension=1, tiled=True)
    squares = jnp.sum(summed * summed, axis=2)
    reduced = lax.psum_scatter(squares, "row", scatter_dimension=0, tiled=True)
    raw_leverage = lax.all_gather(reduced, "feat", axis=1, tiled=True).reshape(rows_dev)
    leverage = raw_leverage / features
    strata_count = 2 * row_count
    membership = (strata[:, None] == jnp.arange(strata_count, dtype=jnp.int32)[None, :]).astype(
        jnp.float32
    )
    products = weights * raw_leverage
    local_product = lax.dot_general(
        membership, products, (((0,), (0,)), ((), ())), precision=lax.Precision.HIGHEST
    )
    local_mass = lax.dot_general(
        membership, weights, (((0,), (0,)), ((), ())), precision=lax.Precision.HIGHEST
    )
    stratum_product, stratum_mass = lax.psum((local_product, local_mass), "row")
    stratum_ratio = stratum_mass / stratum_product
    row_ratio = jnp.dot(membership, stratum_ratio, precision=lax.Precision.HIGHEST)
    new_weight = products * row_ratio
    weight_step = new_weight - weights
    step_all = lax.all_gather(weight_step, "row", axis=0, tiled=True)
    scaled_all = (step_all[:, None] * gathered.astype(jnp.float32)).astype(jnp.bfloat16)
    blocks_per_feat = row_count // feat_count
    row_index = lax.axis_index("row")
    offset = row_index % blocks_per_feat * row_block
    mine = lax.dynamic_slice_in_dim(gathered, offset, row_block, 1)
    root_index = row_index // blocks_per_feat
    column_block = broadcast(mine, "feat", root_index)
    information = lax.dot_general(
        column_block, scaled_all, (((0,), (0,)), ((), ())), preferred_element_type=jnp.float32
    )
    return (new_weight, leverage, information)


def solution(mesh):
    in_specs = (P("row", "feat"), P("row", "feat"), P("row"), P("row"))
    out_specs = (P("row"), P("row"), P("row", "feat"))
    return jax.shard_map(
        per_device, mesh=mesh, in_specs=in_specs, out_specs=out_specs, check_vma=False
    )
```

profile of v0, /device:TPU:0, one launch (start us, length us, event | category | flops | bytes accessed | tf_op | source)
XLA Modules:
  0.0 475.3 jit_solution(4714383224408392123)
XLA Ops:
  7.2 0.0 copy-start
  7.2 0.0 all-gather.2.cloned.1.call-start
  7.2 0.7 all-gather.2.cloned.1.call-update
  7.9 0.0 reduce-scatter.2.cloned.1.call-start
  8.0 102.2 %all-gather.2.cloned.1.call-done = bf16[2048,2048]{1,0:T(8,128)(2,1)} async-done(((bf16[64,2048]{1,0:T(8,128)(2,1)}), bf16[2048,2048]{1,0:T(8,128)(2,1)}) %all-gather.2.cloned.1.call-update) | async-done | bytes 8388624 | tf_op jit(solution)/shard_map/all_gather | solution.py:19
  110.2 0.0 copy-done
  110.2 9.5 %fusion.12 = f32[2048,512]{1,0:T(8,128)} fusion(bf16[2048,2048]{1,0:T(8,128)(2,1)} %all-gather.2.cloned.1.call-done, bf16[512,2048]{1,0:T(8,128)(2,1)S(1)} %copy-done), kind=kOutput, calls=%fused_computation.22 | convolution fusion | flops 4294967296 | bytes 14680064 | tf_op jit(solution)/shard_map/dot_general | solution.py:20
  119.7 0.0 reduce-scatter.2.cloned.1.call-update
  119.7 0.0 copy-start.1
  119.7 0.0 copy-start.4
  119.7 0.0 copy-start.5
  119.7 0.0 copy-start.2
  119.7 0.0 all-reduce.6.cloned.1.call-start
  119.8 3.3 dynamic-slice_select_fusion
  123.1 0.0 all-reduce.6.cloned.1.call-update
  123.1 0.2 convolution_bitcast_fusion.2
  123.3 0.6 dynamic-slice
  124.6 0.6 fusion.11
  125.9 31.5 %reduce-scatter.2.cloned.1.call-done = f32[32,8,512]{2,1,0:T(8,128)} async-done(((f32[32,64,512]{2,1,0:T(8,128)}), f32[32,8,512]{2,1,0:T(8,128)}) %reduce-scatter.2.cloned.1.call-update) | async-done | bytes 524304 | tf_op jit(solution)/shard_map/reduce_scatter | solution.py:24
  157.4 1.2 multiply_reduce_fusion
  158.5 143.1 %all-reduce.2 = f32[32,8]{1,0:T(8,128)S(1)} all-reduce(f32[32,8]{1,0:T(8,128)S(1)} %multiply_reduce_fusion), channel_id=3, replica_groups=mesh['row'=32,'feat'=8] {'row'}, use_global_device_ids=true, to_apply=%region_2.0.clone | all-reduce | flops 256 | bytes 2048
  301.6 0.7 fusion.6
  302.3 12.4 %all-reduce = f32[64]{0:T(128)S(1)} all-reduce(f32[64]{0:T(128)S(1)} %fusion.6), channel_id=1, replica_groups=mesh['row'=32,'feat'=8] {'feat'}, use_global_device_ids=true, to_apply=%add | all-reduce | flops 64 | bytes 512 | tf_op jit(solution)/shard_map/reshape | solution.py:27
  314.7 0.5 broadcast_multiply_fusion
  315.2 0.2 convolution_bitcast_fusion.1
  315.4 69.6 %all-reduce.3 = (f32[64]{0:T(128)S(1)}, f32[64]{0:T(128)S(1)}) all-reduce(f32[64]{0:T(128)S(1)} %convolution_bitcast_fusion.2, f32[64]{0:T(128)S(1)} %convolution_bitcast_fusion.1), channel_id=1, replica_groups=mesh['row'=32,'feat'=8] {'row'}, use_global_device_ids=true, to_apply=%region_3.0 | all-reduce | flops 128 | bytes 1024 | tf_op jit(solution)/shard_map/psum | solution.py:40
  385.0 0.2 fusion.2
  385.2 0.1 subtract_dynamic-update-slice_fusion
  385.4 72.6 %all-reduce.1 = f32[2048]{0:T(1024)S(1)} all-reduce(f32[2048]{0:T(1024)S(1)} %subtract_dynamic-update-slice_fusion), channel_id=1, replica_groups=mesh['row'=32,'feat'=8] {'row'}, use_global_device_ids=true, to_apply=%add.1 | all-reduce | flops 2048 | bytes 16384
  458.0 0.0 all-reduce.6.cloned.1.call-done
  458.0 10.8 %fusion = f32[512,2048]{1,0:T(8,128)} fusion(bf16[2048,512]{1,0:T(8,128)(2,1)} %all-reduce.6.cloned.1.call-done, bf16[2048,2048]{1,0:T(8,128)(2,1)} %all-gather.2.cloned.1.call-done, f32[2048]{0:T(1024)S(1)} %all-reduce.1), kind=kOutput, calls=%fused_computation.1 | convolution fusion | flops 4307550208 | bytes 14688256 | tf_op jit(solution)/shard_map/dot_general | solution.py:53
  468.8 0.0 copy-done.3
  (7 shorter events, 0.0 us)
Async XLA Ops:
  7.2 103.0 %copy-start = (bf16[512,2048]{1,0:T(8,128)(2,1)S(1)}, bf16[512,2048]{1,0:T(8,128)(2,1)}, u32[]{:S(2)}) copy-start(bf16[512,2048]{1,0:T(8,128)(2,1)} %param.5) | copy-start | bytes 6291460
  7.2 103.0 %all-gather.2.cloned.1.call-start = ((), (), s32[]{:S(2)}) async-start(), calls=%async_computation.1 | async-start | bytes 8650752 | tf_op jit(solution)/shard_map/all_gather | solution.py:19
  7.9 149.5 %reduce-scatter.2.cloned.1.call-start = ((), (), s32[]{:S(2)}) async-start(), calls=%async_computation.2 | async-start | bytes 4718592 | tf_op jit(solution)/shard_map/reduce_scatter | solution.py:24
  119.7 3.4 copy-start.1
  119.7 3.4 copy-start.4
  119.7 3.6 copy-start.5
  119.7 4.8 %copy-start.2 = (u32[256]{0:T(256)S(1)}, u32[256]{0:T(256)}, u32[]{:S(2)}) copy-start(u32[256]{0:T(256)} %constant.54) | copy-start | bytes 3076
  119.7 338.3 %all-reduce.6.cloned.1.call-start = ((), (), s32[]{:S(2)}) async-start(), calls=%async_computation.3 | async-start | bytes 4194304 | tf_op jit(solution)/shard_map/psum | solution.py:9
  385.2 83.6 %copy-start.3 = (f32[64]{0:T(128)}, f32[64]{0:T(128)S(1)}, u32[]{:S(2)}) copy-start(f32[64]{0:T(128)S(1)} %fusion.2) | copy-start | bytes 772
Sparse Core Ops, SparseCore 0:
  10.6 99.5 all-gather.1
  119.8 37.5 reduce-scatter.1
  159.7 69.6 all-reduce.5
where the time goes:
time: 476 us; the launch traced here: 475 us
  blocking collectives  298 us (63%)
  waiting for transfers between devices  134 us (28%)
  matrix products  20.8 us (4%)
  between operations  15.2 us (3%)
  other arithmetic  5.06 us (1%)
    unnamed x2, blocking collectives  216 us
    all_gather x1, waiting for transfers between devices, per_device(): gathered = lax.all_gather(candidates, 'row', axis=0, tiled=True)  102 us
    psum x1, blocking collectives, per_device(): stratum_product, stratum_mass = lax.psum((local_product, local_mass), 'row')  69.6 us
    reduce_scatter x1, waiting for transfers between devices, per_device(): summed = lax.psum_scatter(shaped, 'feat', scatter_dimension=1, tiled=True)  31.5 us
    reshape x1, blocking collectives, per_device(): lax.all_gather(reduced, 'feat', axis=1, tiled=True).reshape(rows_dev)  12.4 us
    dot_general x1, matrix products, per_device(): lax.dot_general(column_block, scaled_all, (((0,), (0,)), ((), ())), prefe...  10.8 us
  transfers between devices with their start and end apart: 3, of which 2 were waited for; matrix products, arithmetic and copies ran while one was open for 2% of the time, Pallas kernels for 0%

commit v1 on v0

v1 whole, which is shorter than its diff:
```python
import functools

import jax
import jax.numpy as jnp
from jax import lax
from jax.experimental import pallas as pl
from jax.experimental.pallas import tpu as pltpu
from jax.sharding import PartitionSpec as P

MESH = pl.DeviceIdType.MESH
NX, NY, NZ, NC = 4, 4, 8, 2
STRATA = 64
CUT = 768
OFFSETS = (0, 1, -1, 2, -2, 3, -3, 4)


def gather_kernel(
    cand, fac, wt,
    G, S, nw_ref, lev_ref,
    F, Ci, pb, px, ysb, ysr, V, wx, wz0, wz, lx, lz0, lz, lt0, lt,
    loc_sem, gs, gr, ws, wr, pxs, pxr, yss, ysrs, cs, cr, ls, lr,
):
    features = NY * NC * cand.shape[1]
    row, feat = lax.axis_index("row"), lax.axis_index("feat")
    x, z = row // NZ, row % NZ
    y, c = feat // NC, feat % NC

    def xdev(d):
        return (lax.rem(x + d + NX, NX) * NZ + z, feat)

    def zdev(d):
        return (x * NZ + lax.rem(z + d + NZ, NZ), feat)

    def fdev(dy, dc):
        return (row, lax.rem(y + dy, NY) * NC + lax.rem(c + dc, NC))

    fcopies = [(dy, dc) for dy in range(NY) for dc in range(NC) if (dy, dc) != (0, 0)]

    def xx(d):
        return lax.rem(x + d + NX, NX)

    def zz(d):
        return lax.rem(z + d + NZ, NZ)

    fcopy = pltpu.make_async_copy(fac, F, loc_sem.at[0])
    fcopy.start()
    mine = pltpu.make_async_copy(cand, G.at[x // 2, z, x % 2], loc_sem.at[1])
    mine.start()

    barrier = pltpu.get_barrier_semaphore()
    peers = (
        [xdev(d) for d in range(1, NX)] + [zdev(d) for d in range(1, NZ)] + [fdev(*d) for d in fcopies]
    )
    for dev in peers:
        pl.semaphore_signal(barrier, inc=1, device_id=dev, device_id_type=MESH)
    mine.wait()
    pl.semaphore_wait(barrier, len(peers))

    pending = []

    def remote(src, dst, ssem, rsem, dev):
        cp = pltpu.make_async_remote_copy(
            src_ref=src, dst_ref=dst, send_sem=ssem, recv_sem=rsem, device_id=dev, device_id_type=MESH
        )
        cp.start()
        pending.append(cp)
        return cp

    count = [0]

    def gsend(view, dev):
        k = count[0]
        count[0] += 1
        return remote(view, view, gs.at[k], gr.at[k], dev)

    cols_a, cols_b = pl.ds(0, CUT), pl.ds(CUT, cand.shape[1] - CUT)
    rows_dev = cand.shape[0]
    half = rows_dev // 2
    SIGNS = (1, -1)

    def half_of(s):
        return pl.ds(0 if s > 0 else half, half)

    def chunk(xp, zp, cols, rows=None):
        if rows is None:
            rows = pl.ds(0, rows_dev)
        return G.at[xp // 2, zp, xp % 2, rows, cols]

    def plane(cp, zp):
        return G.at[cp, zp, :, :, cols_a]

    XA1, XA2, ZB, ZA, XB, XH = {}, {}, {}, {}, {}, {}

    def start_xb(o):
        for s in SIGNS:
            XB[o, s] = gsend(chunk(x, zz(o), cols_b), xdev(s))

    def forward_xb(o):
        for s in SIGNS:
            XB[o, s].wait_recv()
            XH[o, s] = gsend(chunk(xx(-s), zz(o), cols_b, half_of(s)), xdev(s))

    def finish_xh(o):
        for s in SIGNS:
            XH[o, s].wait_recv()

    def forward_zb(d):
        for s in SIGNS:
            ZB[d, s].wait_recv()
            if d < 3:
                ZB[d + 1, s] = gsend(chunk(x, zz(-s * d), cols_b), zdev(s))
            elif d == 3:
                ZB[d + 1, s] = gsend(chunk(x, zz(-s * d), cols_b, half_of(s)), zdev(s))

    def forward_za(d):
        for cp in range(2):
            for s in SIGNS:
                if (d, s, cp) not in ZA:
                    continue
                ZA[d, s, cp].wait_recv()
                if d < 3 or (d == 3 and cp == (0 if s > 0 else 1)):
                    ZA[d + 1, s, cp] = gsend(plane(cp, zz(-s * d)), zdev(s))

    def product(o):
        zp = zz(o)
        a = G[:, zp].reshape(NX * rows_dev, cand.shape[1])
        for n in range(2):
            rows = pl.ds(n * 256, 256)
            p = lax.dot_general(
                F[rows, :], a, (((1,), (1,)), ((), ())), preferred_element_type=jnp.float32
            ).astype(jnp.bfloat16)
            pb[zp, 0, rows, :] = p[:, :128]
            pb[zp, 1, rows, :] = p[:, 128:]

    PX, YS = {}, {}

    def send_half(o):
        i = OFFSETS.index(o)
        zp = zz(o)
        PX[o] = remote(pb.at[zp, 1 - c], px.at[zp], pxs.at[i], pxr.at[i], fdev(0, 1))

    def send_quarters(o):
        i = OFFSETS.index(o)
        zp = zz(o)
        PX[o].wait_recv()
        q = pb[zp, c].astype(jnp.float32) + px[zp].astype(jnp.float32)
        ysb[zp] = q.astype(jnp.bfloat16).reshape(NY, 128, 128)
        for d in range(1, NY):
            yp = lax.rem(y + d, NY)
            YS[o, d] = remote(
                ysb.at[zp, yp], ysr.at[zp, d], yss.at[i * 3 + d - 1], ysrs.at[i * 3 + d - 1], fdev(d, 0)
            )

    def squares(o):
        zp = zz(o)
        total = ysb[zp, y].astype(jnp.float32)
        for d in range(1, NY):
            YS[o, d].wait_recv()
            total = total + ysr[zp, d].astype(jnp.float32)
        V[pl.ds(zp, 1), :] = jnp.sum(total * total, axis=0, keepdims=True)

    block = Ci.shape[-1]
    col0 = pl.multiple_of((z % 4) * block, block)
    croot = z // 4
    dy = lax.rem(y - x + NY, NY)
    on_core = c == croot
    is_root = jnp.logical_and(dy == 0, on_core)

    def ci_copy(o, slot, src, dev):
        i = OFFSETS.index(o)
        return pltpu.make_async_remote_copy(
            src_ref=src, dst_ref=Ci.at[:, zz(o)], send_sem=cs.at[i * 3 + slot], recv_sem=cr.at[i],
            device_id=dev, device_id_type=MESH,
        )

    def ci_source(o):
        return G.at[:, zz(o), :, :, pl.ds(col0, block)]

    def ci_root(o):
        @pl.when(is_root)
        def _():
            src = ci_source(o)
            ci_copy(o, 0, src, fdev(1, 0)).start()
            ci_copy(o, 1, src, fdev(3, 0)).start()
            ci_copy(o, 2, src, fdev(0, 1)).start()
            own = pltpu.make_async_copy(src, Ci.at[:, zz(o)], cr.at[OFFSETS.index(o)])
            own.start()
            own.wait()

    def relays(o):
        i = OFFSETS.index(o)
        src = Ci.at[:, zz(o)]
        far = jnp.logical_and(on_core, dy == (1 if i % 2 == 0 else 3))
        far_dev = fdev(1 if i % 2 == 0 else 3, 0)
        near = jnp.logical_and(on_core, dy != 0)
        return src, far, far_dev, near

    def ci_step(o):
        @pl.when(jnp.logical_not(is_root))
        def _():
            ci_copy(o, 0, Ci.at[:, zz(o)], fdev(0, 1)).wait_recv()

        src, far, far_dev, near = relays(o)

        @pl.when(far)
        def _():
            ci_copy(o, 0, src, far_dev).start()

        @pl.when(near)
        def _():
            ci_copy(o, 2, src, fdev(0, 1)).start()

        for cp in range(2):
            t = Ci[cp, zz(o)].reshape(128, block)
            S[:, pl.ds(pl.multiple_of((cp * NZ + zz(o)) * 128, 128), 128)] = t.T

    def ci_finish(o):
        src, far, far_dev, near = relays(o)

        @pl.when(is_root)
        def _():
            for slot in range(3):
                ci_copy(o, slot, ci_source(o), fdev(0, 1)).wait_send()

        @pl.when(far)
        def _():
            ci_copy(o, 0, src, far_dev).wait_send()

        @pl.when(near)
        def _():
            ci_copy(o, 2, src, fdev(0, 1)).wait_send()

    for s in SIGNS:
        XA1[s] = gsend(chunk(x, z, cols_a), xdev(s))
    for s in SIGNS:
        ZB[1, s] = gsend(chunk(x, z, cols_b), zdev(s))
    WX = [remote(wt, wx.at[d], ws.at[d - 1], wr.at[d - 1], xdev(d)) for d in range(1, NX)]
    start_xb(0)
    for s in SIGNS:
        XA1[s].wait_recv()
        XA2[s] = gsend(chunk(xx(-s), z, cols_a, half_of(s)), xdev(s))
    forward_zb(1)
    start_xb(1)
    start_xb(-1)
    forward_xb(0)
    for s in SIGNS:
        XA2[s].wait_recv()
    for cp in range(2):
        for s in SIGNS:
            ZA[1, s, cp] = gsend(plane(cp, z), zdev(s))
    total = wt[...]
    for d in range(1, NX):
        WX[d - 1].wait_recv()
        total = total + wx[d]
    wz0[...] = total
    WZ = [remote(wz0, wz.at[d], ws.at[d + 2], wr.at[d + 2], zdev(d)) for d in range(1, NZ)]
    fcopy.wait()

    forward_zb(2)
    start_xb(2)
    start_xb(-2)
    forward_xb(1)
    forward_xb(-1)
    finish_xh(0)
    product(0)
    send_half(0)
    ci_root(0)
    forward_zb(3)
    start_xb(3)
    start_xb(-3)
    forward_za(1)
    send_quarters(0)
    finish_xh(1)
    finish_xh(-1)
    product(1)
    send_half(1)
    product(-1)
    send_half(-1)
    ci_root(1)
    ci_root(-1)
    ci_step(0)
    forward_xb(2)
    forward_xb(-2)
    forward_zb(4)
    start_xb(4)
    squares(0)
    send_quarters(1)
    send_quarters(-1)
    forward_za(2)
    finish_xh(2)
    finish_xh(-2)
    product(2)
    send_half(2)
    product(-2)
    send_half(-2)
    ci_root(2)
    ci_root(-2)
    ci_step(1)
    ci_step(-1)
    forward_xb(3)
    forward_xb(-3)
    squares(1)
    squares(-1)
    send_quarters(2)
    send_quarters(-2)
    total = wz0[...]
    for d in range(1, NZ):
        WZ[d - 1].wait_recv()
        total = total + wz[d]
    wz0_all = total
    forward_za(3)
    finish_xh(3)
    finish_xh(-3)
    product(3)
    send_half(3)
    product(-3)
    send_half(-3)
    forward_xb(4)
    ci_root(3)
    ci_root(-3)
    squares(2)
    squares(-2)
    send_quarters(3)
    send_quarters(-3)
    ci_step(2)
    ci_step(-2)
    forward_za(4)
    finish_xh(4)
    product(4)
    send_half(4)
    ci_root(4)
    squares(3)
    squares(-3)
    send_quarters(4)
    squares(4)

    v = V[...]
    lx[0] = v
    LX = [remote(lx.at[0], lx.at[d], ls.at[d - 1], lr.at[d - 1], xdev(d)) for d in range(1, NX)]
    ci_step(3)
    ci_step(-3)
    for cp in LX:
        cp.wait_recv()
    lz0[...] = (lx[0] + lx[1]) + (lx[2] + lx[3])
    LZ = [remote(lz0, lz.at[d], ls.at[d + 2], lr.at[d + 2], zdev(d)) for d in range(1, NZ)]
    ci_step(4)
    v = lz0[...]
    for d in range(1, NZ):
        LZ[d - 1].wait_recv()
        v = v + lz[d]
    lt0[...] = v
    LT = [
        remote(lt0, lt.at[k], ls.at[k + 9], lr.at[k + 9], fdev(*d)) for k, d in enumerate(fcopies, 1)
    ]
    weights = [wz0_all[0], wz0_all[1]]
    labels = [wz0_all[2], wz0_all[3]]
    ids = lax.broadcasted_iota(jnp.int32, (STRATA, 128), 0).astype(jnp.float32)

    def over_strata(tiles):
        acc = jnp.zeros((STRATA, 128), jnp.float32)
        for cp in range(2):
            for zp in range(NZ):
                acc = acc + jnp.where(labels[cp][zp : zp + 1, :] == ids, tiles[cp][zp : zp + 1, :], 0.0)
        return jnp.sum(acc, axis=1, keepdims=True)

    mass = over_strata(weights)
    same, other = lt0[...], None
    for k, (dyk, dck) in enumerate(fcopies, 1):
        LT[k - 1].wait_recv()
        if dck == 0:
            same = same + lt[k]
        else:
            other = lt[k] if other is None else other + lt[k]
    first = c == 0
    raw = [jnp.where(first, same, other), jnp.where(first, other, same)]
    products = [weights[cp] * raw[cp] for cp in range(2)]
    ratio = mass / over_strata(products)
    for cp in range(2):
        rows = [
            jnp.sum(jnp.where(labels[cp][zp : zp + 1, :] == ids, ratio, 0.0), axis=0, keepdims=True)
            for zp in range(NZ)
        ]
        row_ratio = jnp.concatenate(rows, axis=0)
        new_weight = products[cp] * row_ratio
        nw_ref[cp] = new_weight
        lev_ref[cp] = raw[cp] / features
        step = new_weight - weights[cp]
        for zp in range(NZ):
            cols = pl.ds((cp * NZ + zp) * 128, 128)
            S[:, cols] = (S[:, cols].astype(jnp.float32) * step[zp : zp + 1, :]).astype(jnp.bfloat16)

    for cp in pending:
        cp.wait_send()
    for o in OFFSETS:
        ci_finish(o)


def gather(cand, fac, wt):
    rows_dev, feat_block = cand.shape
    row_block = fac.shape[0]
    bf, f32 = jnp.bfloat16, jnp.float32
    vmem = pl.BlockSpec(memory_space=pltpu.VMEM)
    anys = pl.BlockSpec(memory_space=pl.ANY)
    dma = pltpu.SemaphoreType.DMA
    return pl.pallas_call(
        gather_kernel,
        out_shape=(
            pltpu.VMEM((2, NZ, 2, rows_dev, feat_block), bf),
            pltpu.VMEM((row_block, NX * NZ * rows_dev), bf),
            jax.ShapeDtypeStruct((2, NZ, 128), f32),
            jax.ShapeDtypeStruct((2, NZ, 128), f32),
        ),
        in_specs=[anys, anys, vmem],
        out_specs=(vmem, vmem, vmem, vmem),
        scratch_shapes=[
            pltpu.VMEM(fac.shape, bf),
            pltpu.VMEM((2, NZ, 2, rows_dev, row_block), bf),
            pltpu.VMEM((NZ, 2, row_block, 128), bf),
            pltpu.VMEM((NZ, row_block, 128), bf),
            pltpu.VMEM((NZ, NY, 128, 128), bf),
            pltpu.VMEM((NZ, NY, 128, 128), bf),
            pltpu.VMEM((NZ, 128), f32),
            pltpu.VMEM((NX, 4, NZ, 128), f32),
            pltpu.VMEM((4, NZ, 128), f32),
            pltpu.VMEM((NZ, 4, NZ, 128), f32),
            pltpu.VMEM((NX, NZ, 128), f32),
            pltpu.VMEM((NZ, 128), f32),
            pltpu.VMEM((NZ, NZ, 128), f32),
            pltpu.VMEM((NZ, 128), f32),
            pltpu.VMEM((NZ, NZ, 128), f32),
            dma((2,)),
            dma((58,)),
            dma((58,)),
            dma((10,)),
            dma((10,)),
            dma((8,)),
            dma((8,)),
            dma((24,)),
            dma((24,)),
            dma((24,)),
            dma((8,)),
            dma((17,)),
            dma((17,)),
        ],
        compiler_params=pltpu.CompilerParams(
            collective_id=0, has_side_effects=True, vmem_limit_bytes=40 * 1024 * 1024
        ),
    )(cand, fac, wt)


def increment_kernel(s_ref, g_ref, o_ref):
    j = pl.program_id(0)
    n = o_ref.shape[1]
    cols = pl.ds(pl.multiple_of(j * n, n), n)
    o_ref[...] = jnp.dot(s_ref[...], g_ref[:, cols], preferred_element_type=jnp.float32)


def increment(s, g):
    rows, depth = s.shape
    columns = g.shape[1]
    width = 256
    vmem = pl.BlockSpec(memory_space=pltpu.VMEM)
    return pl.pallas_call(
        increment_kernel,
        grid=(columns // width,),
        out_shape=jax.ShapeDtypeStruct((rows, columns), jnp.float32),
        in_specs=[vmem, vmem],
        out_specs=pl.BlockSpec((rows, width), lambda j: (0, j)),
        compiler_params=pltpu.CompilerParams(vmem_limit_bytes=24 * 1024 * 1024),
    )(s, g)


def per_device(candidates, inv_factor, weights, strata):
    row = lax.axis_index("row")
    x, z = row // NZ, row % NZ
    at = jnp.logical_and(
        jnp.arange(2)[:, None, None] == x // 2,
        jnp.logical_and(
            jnp.arange(NZ)[None, :, None] == z, jnp.arange(128)[None, None, :] // 64 == x % 2
        ),
    )
    pair = jnp.stack([jnp.tile(weights, 2), jnp.tile(strata.astype(jnp.float32), 2)])
    wt = jnp.where(at[None], pair[:, None, None, :], 0.0).reshape(4, NZ, 128)
    g, s, nw, lev = gather(candidates, inv_factor, wt)
    information = increment(s, g.reshape(-1, g.shape[-1]))
    start = (x // 2, z, (x % 2) * 64)
    new_weight = lax.dynamic_slice(nw, start, (1, 1, 64)).reshape(64)
    leverage = lax.dynamic_slice(lev, start, (1, 1, 64)).reshape(64)
    return (new_weight, leverage, information)


def solution(mesh):
    in_specs = (P("row", "feat"), P("row", "feat"), P("row"), P("row"))
    out_specs = (P("row"), P("row"), P("row", "feat"))
    return jax.shard_map(
        per_device, mesh=mesh, in_specs=in_specs, out_specs=out_specs, check_vma=False
    )
```

time: 476 us -> 117 us (0.25)
  the two profiles are of different devices: /device:TPU:0 before, /device:TPU:1 now
where the time goes in v1:
time: 117 us
  Pallas kernels  111 us (95%)
  local copies, waits for them, and re-layouts  3.97 us (3%)
    pallas_call x1, Pallas kernels, gather(): pl.pallas_call(gather_kernel, out_shape=(pltpu.VMEM((2, NZ, 2, rows_dev,...  105 us
    pallas_call x1, Pallas kernels, increment(): pl.pallas_call(increment_kernel, grid=(columns // width,), out_shape=jax....  6.87 us
    unnamed x4, local copies, waits for them, and re-layouts  2.54 us

profile of v1, /device:TPU:1, one launch (start us, length us, event | category | flops | bytes accessed | tf_op | source)
XLA Modules:
  0.0 117.0 jit_solution(14091372056321424528)
XLA Ops:
  0.7 0.1 broadcast_and_fusion.1
  0.8 0.7 convert_element_type.3
  1.5 0.1 stack_tile.7
  1.6 0.1 broadcast_and_fusion
  1.6 0.7 tile.4
  2.3 0.1 stack_tile.6
  2.4 0.0 copy-start
  2.4 1.6 %copy-done = bf16[512,2048]{1,0:T(8,128)(2,1)S(1)} copy-done((bf16[512,2048]{1,0:T(8,128)(2,1)S(1)}, bf16[512,2048]{1,0:T(8,128)(2,1)}, u32[]{:S(2)}) %copy-start) | copy-done | bytes 2097176
  4.0 0.0 copy-start.1
  4.0 0.9 copy-done.1
  4.9 104.6 %shard_map.67 = (bf16[2,8,2,64,2048]{4,3,2,1,0:T(8,128)(2,1)S(1)}, bf16[512,2048]{1,0:T(8,128)(2,1)S(1)}, f32[2,8,128]{2,1,0:T(8,128)S(1)}, f32[2,8,128]{2,1,0:T(8,128)S(1)}) custom-call(bf16[64,2048]{1,0:T(8,128)(2,1)S(1)} %copy-done.1, bf16[512,2048]{1,0:T(8,128)(2,1)S(1)} %copy-done, f32[4,8,128]{2,1,0:T(8,128)S(1)} %bitcast_select_fusion.wt), custom_call_target="tpu_custom_call" | custom-call | tf_op jit(solution)/shard_map/pallas_call | solution.py:405
  109.5 0.6 dynamic-slice_bitcast_fusion
  110.1 6.9 %shard_map.68 = f32[512,2048]{1,0:T(8,128)} custom-call(bf16[512,2048]{1,0:T(8,128)(2,1)S(1)} %get-tuple-element.9.s_ref, bf16[2048,2048]{1,0:T(8,128)(2,1)S(1)} %bitcast.8), custom_call_target="tpu_custom_call" | custom-call | tf_op jit(solution)/shard_map/pallas_call | solution.py:463
  (7 shorter events, 0.0 us)
Async XLA Ops:
  2.4 1.6 %copy-start = (bf16[512,2048]{1,0:T(8,128)(2,1)S(1)}, bf16[512,2048]{1,0:T(8,128)(2,1)}, u32[]{:S(2)}) copy-start(bf16[512,2048]{1,0:T(8,128)(2,1)} %fac.1) | copy-start | bytes 6291460
  4.0 0.9 copy-start.1

commit v2 on v1

--- a/solution.py
+++ b/solution.py
@@ -15,9 +15,9 @@
 
 
 def gather_kernel(
-    cand, fac, wt,
+    cand, fac, w_hbm, st_hbm,
     G, S, nw_ref, lev_ref,
-    F, Ci, pb, px, ysb, ysr, V, wx, wz0, wz, lx, lz0, lz, lt0, lt,
+    w_ref, st_ref, twice, wt, F, Ci, pb, px, ysb, ysr, V, wx, wz0, wz, lx, lz0, lz, lt0, lt,
     loc_sem, gs, gr, ws, wr, pxs, pxr, yss, ysrs, cs, cr, ls, lr,
 ):
     features = NY * NC * cand.shape[1]
@@ -43,9 +43,15 @@
         return lax.rem(z + d + NZ, NZ)
 
     fcopy = pltpu.make_async_copy(fac, F, loc_sem.at[0])
-    fcopy.start()
+    smalls = [
+        pltpu.make_async_copy(w_hbm, w_ref, loc_sem.at[2]),
+        pltpu.make_async_copy(st_hbm, st_ref, loc_sem.at[3]),
+    ]
     mine = pltpu.make_async_copy(cand, G.at[x // 2, z, x % 2], loc_sem.at[1])
     mine.start()
+    for cp in smalls:
+        cp.start()
+    fcopy.start()
 
     barrier = pltpu.get_barrier_semaphore()
     peers = (
@@ -53,6 +59,20 @@
     )
     for dev in peers:
         pl.semaphore_signal(barrier, inc=1, device_id=dev, device_id_type=MESH)
+    for cp in smalls:
+        cp.wait()
+    twice[0:1, 0:64] = w_ref[...]
+    twice[0:1, 64:128] = w_ref[...]
+    twice[1:2, 0:64] = st_ref[...].astype(jnp.float32)
+    twice[1:2, 64:128] = st_ref[...].astype(jnp.float32)
+    sub = lax.broadcasted_iota(jnp.int32, (NZ, 128), 0)
+    lane = lax.broadcasted_iota(jnp.int32, (NZ, 128), 1)
+    here = jnp.logical_and(sub == z, lane // 64 == x % 2)
+    for k in range(2):
+        placed = jnp.where(here, twice[k : k + 1, :], 0.0)
+        for cp in range(2):
+            wt[2 * k + cp] = jnp.where(x // 2 == cp, placed, 0.0)
+
     mine.wait()
     pl.semaphore_wait(barrier, len(peers))
 
@@ -187,48 +207,48 @@
             own.start()
             own.wait()
 
-    def relays(o):
+    def ci_wait(o):
+        ci_copy(o, 0, Ci.at[:, zz(o)], fdev(0, 1)).wait_recv()
+
+    def ci_near(o):
         i = OFFSETS.index(o)
-        src = Ci.at[:, zz(o)]
-        far = jnp.logical_and(on_core, dy == (1 if i % 2 == 0 else 3))
-        far_dev = fdev(1 if i % 2 == 0 else 3, 0)
-        near = jnp.logical_and(on_core, dy != 0)
-        return src, far, far_dev, near
-
-    def ci_step(o):
-        @pl.when(jnp.logical_not(is_root))
+        for d in (1, 3):
+            @pl.when(jnp.logical_and(on_core, dy == d))
+            def _():
+                ci_wait(o)
+                if d == (1 if i % 2 == 0 else 3):
+                    ci_copy(o, 0, Ci.at[:, zz(o)], fdev(d, 0)).start()
+                ci_copy(o, 2, Ci.at[:, zz(o)], fdev(0, 1)).start()
+
+    def ci_far(o):
+        @pl.when(jnp.logical_and(on_core, dy == 2))
         def _():
-            ci_copy(o, 0, Ci.at[:, zz(o)], fdev(0, 1)).wait_recv()
-
-        src, far, far_dev, near = relays(o)
-
-        @pl.when(far)
+            ci_wait(o)
+            ci_copy(o, 2, Ci.at[:, zz(o)], fdev(0, 1)).start()
+
+    def ci_last(o):
+        @pl.when(jnp.logical_not(on_core))
         def _():
-            ci_copy(o, 0, src, far_dev).start()
-
-        @pl.when(near)
-        def _():
-            ci_copy(o, 2, src, fdev(0, 1)).start()
+            ci_wait(o)
 
         for cp in range(2):
             t = Ci[cp, zz(o)].reshape(128, block)
             S[:, pl.ds(pl.multiple_of((cp * NZ + zz(o)) * 128, 128), 128)] = t.T
 
     def ci_finish(o):
-        src, far, far_dev, near = relays(o)
+        i = OFFSETS.index(o)
 
         @pl.when(is_root)
         def _():
             for slot in range(3):
                 ci_copy(o, slot, ci_source(o), fdev(0, 1)).wait_send()
 
-        @pl.when(far)
-        def _():
-            ci_copy(o, 0, src, far_dev).wait_send()
-
-        @pl.when(near)
-        def _():
-            ci_copy(o, 2, src, fdev(0, 1)).wait_send()
+        for d in (1, 2, 3):
+            @pl.when(jnp.logical_and(on_core, dy == d))
+            def _():
+                if d == (1 if i % 2 == 0 else 3):
+                    ci_copy(o, 0, Ci.at[:, zz(o)], fdev(0, 1)).wait_send()
+                ci_copy(o, 2, Ci.at[:, zz(o)], fdev(0, 1)).wait_send()
 
     for s in SIGNS:
         XA1[s] = gsend(chunk(x, z, cols_a), xdev(s))
@@ -278,7 +298,7 @@
     send_half(-1)
     ci_root(1)
     ci_root(-1)
-    ci_step(0)
+    ci_near(0)
     forward_xb(2)
     forward_xb(-2)
     forward_zb(4)
@@ -295,8 +315,9 @@
     send_half(-2)
     ci_root(2)
     ci_root(-2)
-    ci_step(1)
-    ci_step(-1)
+    ci_far(0)
+    ci_near(1)
+    ci_near(-1)
     forward_xb(3)
     forward_xb(-3)
     squares(1)
@@ -322,8 +343,10 @@
     squares(-2)
     send_quarters(3)
     send_quarters(-3)
-    ci_step(2)
-    ci_step(-2)
+    ci_far(1)
+    ci_far(-1)
+    ci_near(2)
+    ci_near(-2)
     forward_za(4)
     finish_xh(4)
     product(4)
@@ -332,18 +355,26 @@
     squares(3)
     squares(-3)
     send_quarters(4)
+    for o in (0, 1, -1):
+        ci_last(o)
     squares(4)
 
     v = V[...]
     lx[0] = v
     LX = [remote(lx.at[0], lx.at[d], ls.at[d - 1], lr.at[d - 1], xdev(d)) for d in range(1, NX)]
-    ci_step(3)
-    ci_step(-3)
+    for o in (2, -2):
+        ci_far(o)
+    for o in (3, -3):
+        ci_near(o)
     for cp in LX:
         cp.wait_recv()
     lz0[...] = (lx[0] + lx[1]) + (lx[2] + lx[3])
     LZ = [remote(lz0, lz.at[d], ls.at[d + 2], lr.at[d + 2], zdev(d)) for d in range(1, NZ)]
-    ci_step(4)
+    ci_near(4)
+    for o in (3, -3):
+        ci_far(o)
+    for o in (2, -2):
+        ci_last(o)
     v = lz0[...]
     for d in range(1, NZ):
         LZ[d - 1].wait_recv()
@@ -364,6 +395,9 @@
         return jnp.sum(acc, axis=1, keepdims=True)
 
     mass = over_strata(weights)
+    ci_far(4)
+    for o in (3, -3, 4):
+        ci_last(o)
     same, other = lt0[...], None
     for k, (dyk, dck) in enumerate(fcopies, 1):
         LT[k - 1].wait_recv()
@@ -375,6 +409,7 @@
     raw = [jnp.where(first, same, other), jnp.where(first, other, same)]
     products = [weights[cp] * raw[cp] for cp in range(2)]
     ratio = mass / over_strata(products)
+    new_weights = []
     for cp in range(2):
         rows = [
             jnp.sum(jnp.where(labels[cp][zp : zp + 1, :] == ids, ratio, 0.0), axis=0, keepdims=True)
@@ -382,37 +417,48 @@
         ]
         row_ratio = jnp.concatenate(rows, axis=0)
         new_weight = products[cp] * row_ratio
-        nw_ref[cp] = new_weight
-        lev_ref[cp] = raw[cp] / features
+        new_weights.append(new_weight)
         step = new_weight - weights[cp]
         for zp in range(NZ):
             cols = pl.ds((cp * NZ + zp) * 128, 128)
             S[:, cols] = (S[:, cols].astype(jnp.float32) * step[zp : zp + 1, :]).astype(jnp.bfloat16)
 
+    def own_rows(tiles):
+        tile = jnp.where(x // 2 == 0, tiles[0], tiles[1])
+        line = jnp.sum(jnp.where(sub == z, tile, 0.0), axis=0, keepdims=True)
+        return jnp.where(x % 2 == 0, line[:, :64], line[:, 64:])
+
+    nw_ref[...] = own_rows(new_weights)
+    lev_ref[...] = own_rows(raw) / features
+
     for cp in pending:
         cp.wait_send()
     for o in OFFSETS:
         ci_finish(o)
 
 
-def gather(cand, fac, wt):
+def gather(cand, fac, weights, strata):
     rows_dev, feat_block = cand.shape
     row_block = fac.shape[0]
     bf, f32 = jnp.bfloat16, jnp.float32
     vmem = pl.BlockSpec(memory_space=pltpu.VMEM)
-    anys = pl.BlockSpec(memory_space=pl.ANY)
+    hbm = pl.BlockSpec(memory_space=pltpu.HBM)
     dma = pltpu.SemaphoreType.DMA
     return pl.pallas_call(
         gather_kernel,
         out_shape=(
             pltpu.VMEM((2, NZ, 2, rows_dev, feat_block), bf),
             pltpu.VMEM((row_block, NX * NZ * rows_dev), bf),
-            jax.ShapeDtypeStruct((2, NZ, 128), f32),
-            jax.ShapeDtypeStruct((2, NZ, 128), f32),
+            pltpu.VMEM((1, rows_dev), f32),
+            pltpu.VMEM((1, rows_dev), f32),
         ),
-        in_specs=[anys, anys, vmem],
+        in_specs=[hbm, hbm, hbm, hbm],
         out_specs=(vmem, vmem, vmem, vmem),
         scratch_shapes=[
+            pltpu.VMEM((1, rows_dev), f32),
+            pltpu.VMEM((1, rows_dev), jnp.int32),
+            pltpu.VMEM((8, 128), f32),
+            pltpu.VMEM((4, NZ, 128), f32),
             pltpu.VMEM(fac.shape, bf),
             pltpu.VMEM((2, NZ, 2, rows_dev, row_block), bf),
             pltpu.VMEM((NZ, 2, row_block, 128), bf),
@@ -428,7 +474,7 @@
             pltpu.VMEM((NZ, NZ, 128), f32),
             pltpu.VMEM((NZ, 128), f32),
             pltpu.VMEM((NZ, NZ, 128), f32),
-            dma((2,)),
+            dma((4,)),
             dma((58,)),
             dma((58,)),
             dma((10,)),
@@ -445,48 +491,55 @@
         compiler_params=pltpu.CompilerParams(
             collective_id=0, has_side_effects=True, vmem_limit_bytes=40 * 1024 * 1024
         ),
-    )(cand, fac, wt)
-
-
-def increment_kernel(s_ref, g_ref, o_ref):
-    j = pl.program_id(0)
-    n = o_ref.shape[1]
-    cols = pl.ds(pl.multiple_of(j * n, n), n)
-    o_ref[...] = jnp.dot(s_ref[...], g_ref[:, cols], preferred_element_type=jnp.float32)
-
-
-def increment(s, g):
-    rows, depth = s.shape
+    )(*[
+        pltpu.with_memory_space_constraint(a, pltpu.HBM)
+        for a in (cand, fac, weights.reshape(1, rows_dev), strata.reshape(1, rows_dev))
+    ])
+
+
+WIDTH = 512
+
+
+def increment_kernel(s_ref, g_ref, nw_ref, lev_ref, o_hbm, nw_hbm, lev_hbm, out, sem):
+    copies = [
+        pltpu.make_async_copy(nw_ref, nw_hbm, sem.at[0]),
+        pltpu.make_async_copy(lev_ref, lev_hbm, sem.at[1]),
+    ]
+    for cp in copies:
+        cp.start()
+    for j in range(out.shape[1] // WIDTH):
+        cols = pl.ds(j * WIDTH, WIDTH)
+        out[:, cols] = jnp.dot(s_ref[...], g_ref[:, cols], preferred_element_type=jnp.float32)
+        cp = pltpu.make_async_copy(out.at[:, cols], o_hbm.at[:, cols], sem.at[2 + j])
+        cp.start()
+        copies.append(cp)
+    for cp in copies:
+        cp.wait()
+
+
+def increment(s, g, nw, lev):
+    rows = s.shape[0]
     columns = g.shape[1]
-    width = 256
     vmem = pl.BlockSpec(memory_space=pltpu.VMEM)
+    hbm = pl.BlockSpec(memory_space=pltpu.HBM)
+    f32 = jnp.float32
     return pl.pallas_call(
         increment_kernel,
-        grid=(columns // width,),
-        out_shape=jax.ShapeDtypeStruct((rows, columns), jnp.float32),
-        in_specs=[vmem, vmem],
-        out_specs=pl.BlockSpec((rows, width), lambda j: (0, j)),
-        compiler_params=pltpu.CompilerParams(vmem_limit_bytes=24 * 1024 * 1024),
-    )(s, g)
+        out_shape=(pltpu.HBM((rows, columns), f32), pltpu.HBM(nw.shape, f32), pltpu.HBM(lev.shape, f32)),
+        in_specs=[vmem] * 4,
+        out_specs=(hbm,) * 3,
+        scratch_shapes=[
+            pltpu.VMEM((rows, columns), f32),
+            pltpu.SemaphoreType.DMA((2 + columns // WIDTH,)),
+        ],
+        compiler_params=pltpu.CompilerParams(vmem_limit_bytes=30 * 1024 * 1024),
+    )(s, g, nw, lev)
 
 
 def per_device(candidates, inv_factor, weights, strata):
-    row = lax.axis_index("row")
-    x, z = row // NZ, row % NZ
-    at = jnp.logical_and(
-        jnp.arange(2)[:, None, None] == x // 2,
-        jnp.logical_and(
-            jnp.arange(NZ)[None, :, None] == z, jnp.arange(128)[None, None, :] // 64 == x % 2
-        ),
-    )
-    pair = jnp.stack([jnp.tile(weights, 2), jnp.tile(strata.astype(jnp.float32), 2)])
-    wt = jnp.where(at[None], pair[:, None, None, :], 0.0).reshape(4, NZ, 128)
-    g, s, nw, lev = gather(candidates, inv_factor, wt)
-    information = increment(s, g.reshape(-1, g.shape[-1]))
-    start = (x // 2, z, (x % 2) * 64)
-    new_weight = lax.dynamic_slice(nw, start, (1, 1, 64)).reshape(64)
-    leverage = lax.dynamic_slice(lev, start, (1, 1, 64)).reshape(64)
-    return (new_weight, leverage, information)
+    g, s, nw, lev = gather(candidates, inv_factor, weights, strata)
+    information, nw, lev = increment(s, g.reshape(-1, g.shape[-1]), nw, lev)
+    return (nw.reshape(weights.shape), lev.reshape(weights.shape), information)
 
 
 def solution(mesh):

time: 117 us -> 98.4 us (0.84)
  Pallas kernels: 111 us -> 97.7 us
  local copies, waits for them, and re-layouts: 3.97 us -> 0 us
    pallas_call x1, Pallas kernels: 105 us -> 92.1 us  [gather(): pl.pallas_call(gather_kernel, out_shape=(pltpu.VMEM((2, NZ, 2, rows_dev,...]
    unnamed x4 -> x0, local copies, waits for them, and re-layouts: 2.54 us -> none
    pallas_call x1, Pallas kernels: 6.87 us -> 5.52 us  [increment(): pl.pallas_call(increment_kernel, out_shape=(pltpu.HBM((rows, columns), f3...]
where the time goes in v2:
time: 98.4 us; the launch traced here: 98.3 us
  Pallas kernels  97.7 us (99%)
    pallas_call x1, Pallas kernels, gather(): pl.pallas_call(gather_kernel, out_shape=(pltpu.VMEM((2, NZ, 2, rows_dev,...  92.1 us
    pallas_call x1, Pallas kernels, increment(): pl.pallas_call(increment_kernel, out_shape=(pltpu.HBM((rows, columns), f3...  5.52 us

profile of v2, /device:TPU:1, one launch (start us, length us, event | category | flops | bytes accessed | tf_op | source)
XLA Modules:
  0.0 98.3 jit_solution(5709864947462300779)
XLA Ops:
  0.6 92.1 %shard_map.67 = (bf16[2,8,2,64,2048]{4,3,2,1,0:T(8,128)(2,1)S(1)}, bf16[512,2048]{1,0:T(8,128)(2,1)S(1)}, f32[1,64]{1,0:T(1,128)S(1)}, f32[1,64]{1,0:T(1,128)S(1)}) custom-call(bf16[64,2048]{1,0:T(8,128)(2,1)} %cand.1, bf16[512,2048]{1,0:T(8,128)(2,1)} %fac.1, f32[1,64]{1,0:T(1,128)} %bitcast.6, s32[1,64]{1,0:T(1,128)} %bitcast.7), custom_call_target="tpu_custom_call" | custom-call | tf_op jit(solution)/shard_map/pallas_call | solution.py:447
  92.8 5.5 %shard_map.68 = (f32[512,2048]{1,0:T(8,128)}, f32[1,64]{1,0:T(1,128)}, f32[1,64]{1,0:T(1,128)}) custom-call(bf16[512,2048]{1,0:T(8,128)(2,1)S(1)} %get-tuple-element.10.s_ref, bf16[2048,2048]{1,0:T(8,128)(2,1)S(1)} %bitcast.5, f32[1,64]{1,0:T(1,128)S(1)} %get-tuple-element.12.nw_ref, f32[1,64]{1,0:T(1,128)S(1)} %get-tuple-element.13.lev_ref), custom_call_target="tpu_custom_call" | custom-call | tf_op jit(solution)/shard_map/pallas_call | solution.py:526

commit v3 on v2

--- a/solution.py
+++ b/solution.py
@@ -17,7 +17,7 @@
 def gather_kernel(
     cand, fac, w_hbm, st_hbm,
     G, S, nw_ref, lev_ref,
-    w_ref, st_ref, twice, wt, F, Ci, pb, px, ysb, ysr, V, wx, wz0, wz, lx, lz0, lz, lt0, lt,
+    w_ref, st_ref, twice, wt, F, Ci, pb, px, ysb, ysr, V, wx, wz0, wz, lz0, lz, lt0, lt,
     loc_sem, gs, gr, ws, wr, pxs, pxr, yss, ysrs, cs, cr, ls, lr,
 ):
     features = NY * NC * cand.shape[1]
@@ -34,6 +34,10 @@
     def fdev(dy, dc):
         return (row, lax.rem(y + dy, NY) * NC + lax.rem(c + dc, NC))
 
+    plane_peers = sorted(
+        ((dx, dz) for dx in range(NX) for dz in range(NZ) if (dx, dz) != (0, 0)),
+        key=lambda d: -(min(d[0], NX - d[0]) + min(d[1], NZ - d[1])),
+    )
     fcopies = [(dy, dc) for dy in range(NY) for dc in range(NC) if (dy, dc) != (0, 0)]
 
     def xx(d):
@@ -54,9 +58,7 @@
     fcopy.start()
 
     barrier = pltpu.get_barrier_semaphore()
-    peers = (
-        [xdev(d) for d in range(1, NX)] + [zdev(d) for d in range(1, NZ)] + [fdev(*d) for d in fcopies]
-    )
+    peers = [xdev(1), xdev(-1), zdev(1), zdev(-1), fdev(0, 1)] + [fdev(d, 0) for d in range(1, NY)]
     for dev in peers:
         pl.semaphore_signal(barrier, inc=1, device_id=dev, device_id_type=MESH)
     for cp in smalls:
@@ -78,12 +80,13 @@
 
     pending = []
 
-    def remote(src, dst, ssem, rsem, dev):
+    def remote(src, dst, ssem, rsem, dev, keep=True):
         cp = pltpu.make_async_remote_copy(
             src_ref=src, dst_ref=dst, send_sem=ssem, recv_sem=rsem, device_id=dev, device_id_type=MESH
         )
         cp.start()
-        pending.append(cp)
+        if keep:
+            pending.append(cp)
         return cp
 
     count = [0]
@@ -254,7 +257,6 @@
         XA1[s] = gsend(chunk(x, z, cols_a), xdev(s))
     for s in SIGNS:
         ZB[1, s] = gsend(chunk(x, z, cols_b), zdev(s))
-    WX = [remote(wt, wx.at[d], ws.at[d - 1], wr.at[d - 1], xdev(d)) for d in range(1, NX)]
     start_xb(0)
     for s in SIGNS:
         XA1[s].wait_recv()
@@ -268,12 +270,7 @@
     for cp in range(2):
         for s in SIGNS:
             ZA[1, s, cp] = gsend(plane(cp, z), zdev(s))
-    total = wt[...]
-    for d in range(1, NX):
-        WX[d - 1].wait_recv()
-        total = total + wx[d]
-    wz0[...] = total
-    WZ = [remote(wz0, wz.at[d], ws.at[d + 2], wr.at[d + 2], zdev(d)) for d in range(1, NZ)]
+    WX = [remote(wt, wx.at[d], ws.at[d - 1], wr.at[d - 1], xdev(d)) for d in range(1, NX)]
     fcopy.wait()
 
     forward_zb(2)
@@ -282,9 +279,9 @@
     forward_xb(1)
     forward_xb(-1)
     finish_xh(0)
+    ci_root(0)
     product(0)
     send_half(0)
-    ci_root(0)
     forward_zb(3)
     start_xb(3)
     start_xb(-3)
@@ -292,29 +289,35 @@
     send_quarters(0)
     finish_xh(1)
     finish_xh(-1)
+    ci_root(1)
+    ci_root(-1)
     product(1)
     send_half(1)
     product(-1)
     send_half(-1)
-    ci_root(1)
-    ci_root(-1)
     ci_near(0)
     forward_xb(2)
     forward_xb(-2)
     forward_zb(4)
     start_xb(4)
+    total = wt[...]
+    for d in range(1, NX):
+        WX[d - 1].wait_recv()
+        total = total + wx[d]
+    wz0[...] = total
+    WZ = [remote(wz0, wz.at[d], ws.at[d + 2], wr.at[d + 2], zdev(d)) for d in range(1, NZ)]
     squares(0)
     send_quarters(1)
     send_quarters(-1)
     forward_za(2)
     finish_xh(2)
     finish_xh(-2)
+    ci_root(2)
+    ci_root(-2)
     product(2)
     send_half(2)
     product(-2)
     send_half(-2)
-    ci_root(2)
-    ci_root(-2)
     ci_far(0)
     ci_near(1)
     ci_near(-1)
@@ -324,21 +327,16 @@
     squares(-1)
     send_quarters(2)
     send_quarters(-2)
-    total = wz0[...]
-    for d in range(1, NZ):
-        WZ[d - 1].wait_recv()
-        total = total + wz[d]
-    wz0_all = total
     forward_za(3)
     finish_xh(3)
     finish_xh(-3)
+    ci_root(3)
+    ci_root(-3)
     product(3)
     send_half(3)
     product(-3)
     send_half(-3)
     forward_xb(4)
-    ci_root(3)
-    ci_root(-3)
     squares(2)
     squares(-2)
     send_quarters(3)
@@ -348,37 +346,39 @@
     ci_near(2)
     ci_near(-2)
     forward_za(4)
+    total = wz0[...]
+    for d in range(1, NZ):
+        WZ[d - 1].wait_recv()
+        total = total + wz[d]
+    wz0_all = total
     finish_xh(4)
     product(4)
     send_half(4)
+    send_quarters(4)
     ci_root(4)
     squares(3)
     squares(-3)
-    send_quarters(4)
     for o in (0, 1, -1):
         ci_last(o)
     squares(4)
 
-    v = V[...]
-    lx[0] = v
-    LX = [remote(lx.at[0], lx.at[d], ls.at[d - 1], lr.at[d - 1], xdev(d)) for d in range(1, NX)]
+    lz0[...] = V[...]
+    for k, (dx, dz) in enumerate(plane_peers):
+        remote(lz0, lz.at[k], ls.at[0], lr.at[0], (xx(dx) * NZ + zz(dz), feat), keep=False)
+    all_sums = pltpu.make_async_remote_copy(
+        src_ref=lz, dst_ref=lz, send_sem=ls.at[0], recv_sem=lr.at[0], device_id=xdev(1), device_id_type=MESH
+    )
     for o in (2, -2):
         ci_far(o)
     for o in (3, -3):
         ci_near(o)
-    for cp in LX:
-        cp.wait_recv()
-    lz0[...] = (lx[0] + lx[1]) + (lx[2] + lx[3])
-    LZ = [remote(lz0, lz.at[d], ls.at[d + 2], lr.at[d + 2], zdev(d)) for d in range(1, NZ)]
     ci_near(4)
-    for o in (3, -3):
-        ci_far(o)
     for o in (2, -2):
         ci_last(o)
     v = lz0[...]
-    for d in range(1, NZ):
-        LZ[d - 1].wait_recv()
-        v = v + lz[d]
+    all_sums.wait_recv()
+    for k in range(len(plane_peers)):
+        v = v + lz[k]
     lt0[...] = v
     LT = [
         remote(lt0, lt.at[k], ls.at[k + 9], lr.at[k + 9], fdev(*d)) for k, d in enumerate(fcopies, 1)
@@ -395,9 +395,15 @@
         return jnp.sum(acc, axis=1, keepdims=True)
 
     mass = over_strata(weights)
-    ci_far(4)
+    all_sums.wait_send()
+    for o in (3, -3, 4):
+        ci_far(o)
     for o in (3, -3, 4):
         ci_last(o)
+    for cp in pending:
+        cp.wait_send()
+    for o in OFFSETS:
+        ci_finish(o)
     same, other = lt0[...], None
     for k, (dyk, dck) in enumerate(fcopies, 1):
         LT[k - 1].wait_recv()
@@ -430,11 +436,6 @@
 
     nw_ref[...] = own_rows(new_weights)
     lev_ref[...] = own_rows(raw) / features
-
-    for cp in pending:
-        cp.wait_send()
-    for o in OFFSETS:
-        ci_finish(o)
 
 
 def gather(cand, fac, weights, strata):
@@ -469,9 +470,8 @@
             pltpu.VMEM((NX, 4, NZ, 128), f32),
             pltpu.VMEM((4, NZ, 128), f32),
             pltpu.VMEM((NZ, 4, NZ, 128), f32),
-            pltpu.VMEM((NX, NZ, 128), f32),
             pltpu.VMEM((NZ, 128), f32),
-            pltpu.VMEM((NZ, NZ, 128), f32),
+            pltpu.VMEM((NX * NZ - 1, NZ, 128), f32),
             pltpu.VMEM((NZ, 128), f32),
             pltpu.VMEM((NZ, NZ, 128), f32),
             dma((4,)),

time: 98.4 us -> 89.1 us (0.905)
  Pallas kernels: 97.7 us -> 88.2 us
    pallas_call x1, Pallas kernels: 92.1 us -> 82.7 us  [gather(): pl.pallas_call(gather_kernel, out_shape=(pltpu.VMEM((2, NZ, 2, rows_dev,...]
where the time goes in v3:
time: 89.1 us; the launch traced here: 88.9 us
  Pallas kernels  88.2 us (99%)
    pallas_call x1, Pallas kernels, gather(): pl.pallas_call(gather_kernel, out_shape=(pltpu.VMEM((2, NZ, 2, rows_dev,...  82.7 us
    pallas_call x1, Pallas kernels, increment(): pl.pallas_call(increment_kernel, out_shape=(pltpu.HBM((rows, columns), f3...  5.52 us

profile of v3, /device:TPU:1, one launch (start us, length us, event | category | flops | bytes accessed | tf_op | source)
XLA Modules:
  0.0 88.9 jit_solution(8569699242148285348)
XLA Ops:
  0.6 82.7 %shard_map.67 = (bf16[2,8,2,64,2048]{4,3,2,1,0:T(8,128)(2,1)S(1)}, bf16[512,2048]{1,0:T(8,128)(2,1)S(1)}, f32[1,64]{1,0:T(1,128)S(1)}, f32[1,64]{1,0:T(1,128)S(1)}) custom-call(bf16[64,2048]{1,0:T(8,128)(2,1)} %cand.1, bf16[512,2048]{1,0:T(8,128)(2,1)} %fac.1, f32[1,64]{1,0:T(1,128)} %bitcast.6, s32[1,64]{1,0:T(1,128)} %bitcast.7), custom_call_target="tpu_custom_call" | custom-call | tf_op jit(solution)/shard_map/pallas_call | solution.py:448
  83.3 5.5 %shard_map.68 = (f32[512,2048]{1,0:T(8,128)}, f32[1,64]{1,0:T(1,128)}, f32[1,64]{1,0:T(1,128)}) custom-call(bf16[512,2048]{1,0:T(8,128)(2,1)S(1)} %get-tuple-element.10.s_ref, bf16[2048,2048]{1,0:T(8,128)(2,1)S(1)} %bitcast.5, f32[1,64]{1,0:T(1,128)S(1)} %get-tuple-element.12.nw_ref, f32[1,64]{1,0:T(1,128)S(1)} %get-tuple-element.13.lev_ref), custom_call_target="tpu_custom_call" | custom-call | tf_op jit(solution)/shard_map/pallas_call | solution.py:526

commit v4 on v3

--- a/solution.py
+++ b/solution.py
@@ -10,8 +10,26 @@
 MESH = pl.DeviceIdType.MESH
 NX, NY, NZ, NC = 4, 4, 8, 2
 STRATA = 64
-CUT = 768
 OFFSETS = (0, 1, -1, 2, -2, 3, -3, 4)
+CUT_OWN, CUT_NEXT, CUT_FAR = 896, 768, 896
+XA1, XA2, ZB, XB, XH, ZA, PRODUCT, QUARTERS, SQUARES, NEAR, FAR = range(11)
+ORDER = (
+    (ZB, 1, -1), (ZB, 1, 1), (XA1, -1), (XA1, 1), (XB, 0, -1), (XB, 0, 1), (ZA, 1, -1, 0), (ZA, 1, 1, 0),
+    (XA2, -1), (ZA, 1, -1, 1), (XA2, 1), (ZA, 1, 1, 1), (ZA, 1, -1, -1), (ZA, 1, 1, -1), (XB, 1, -1),
+    (XB, 1, 1), (ZB, 2, -1), (ZB, 2, 1), (XB, -1, -1), (XB, -1, 1), (ZA, 1, -1, 2), (ZA, 1, 1, 2),
+    (XH, 0, -1), (XH, 0, 1), (ZA, 2, -1, 0), (ZA, 2, 1, 0), (XH, 1, -1), (XH, 1, 1), (ZA, 2, -1, 1),
+    (ZA, 2, 1, 1), (XB, 2, -1), (XB, 2, 1), (ZB, 3, -1), (ZB, 3, 1), (XH, -1, -1), (XH, -1, 1), (PRODUCT, 0),
+    (XB, -2, -1), (XB, -2, 1), (PRODUCT, 1), (ZA, 2, -1, -1), (ZA, 2, 1, -1), (QUARTERS, 0), (QUARTERS, 1),
+    (ZA, 2, -1, 2), (ZA, 2, 1, 2), (XH, 2, -1), (XH, 2, 1), (SQUARES, 0), (PRODUCT, -1), (ZA, 3, -1, 0),
+    (ZA, 3, 1, 0), (SQUARES, 1), (XB, 3, -1), (XB, 3, 1), (QUARTERS, -1), (NEAR, 0), (ZB, 4, -1), (ZB, 4, 1),
+    (XB, -3, -1), (XB, -3, 1), (NEAR, 1), (ZA, 3, -1, 1), (ZA, 3, 1, 1), (SQUARES, -1), (PRODUCT, 2),
+    (ZA, 3, -1, -1), (ZA, 3, 1, -1), (XH, -2, -1), (XH, -2, 1), (QUARTERS, 2), (ZA, 3, -1, 2), (ZA, 3, 1, 2),
+    (NEAR, -1), (XH, 3, -1), (XH, 3, 1), (XB, 4, -1), (XB, 4, 1), (ZA, 4, 1, 0), (SQUARES, 2), (FAR, 0),
+    (ZA, 4, 1, 1), (FAR, 1), (XH, -3, -1), (XH, -3, 1), (PRODUCT, -2), (ZA, 4, -1, -1), (NEAR, 2),
+    (QUARTERS, -2), (ZA, 4, -1, 2), (PRODUCT, 3), (FAR, -1), (QUARTERS, 3), (XH, 4, -1), (XH, 4, 1),
+    (SQUARES, -2), (PRODUCT, -3), (SQUARES, 3), (QUARTERS, -3), (PRODUCT, 4), (QUARTERS, 4), (SQUARES, -3),
+    (SQUARES, 4),
+)
 
 
 def gather_kernel(
@@ -96,53 +114,57 @@
         count[0] += 1
         return remote(view, view, gs.at[k], gr.at[k], dev)
 
-    cols_a, cols_b = pl.ds(0, CUT), pl.ds(CUT, cand.shape[1] - CUT)
+    columns = cand.shape[1]
     rows_dev = cand.shape[0]
     half = rows_dev // 2
-    SIGNS = (1, -1)
-
-    def half_of(s):
-        return pl.ds(0 if s > 0 else half, half)
-
-    def chunk(xp, zp, cols, rows=None):
-        if rows is None:
-            rows = pl.ds(0, rows_dev)
-        return G.at[xp // 2, zp, xp % 2, rows, cols]
-
-    def plane(cp, zp):
-        return G.at[cp, zp, :, :, cols_a]
-
-    XA1, XA2, ZB, ZA, XB, XH = {}, {}, {}, {}, {}, {}
-
-    def start_xb(o):
-        for s in SIGNS:
-            XB[o, s] = gsend(chunk(x, zz(o), cols_b), xdev(s))
-
-    def forward_xb(o):
-        for s in SIGNS:
-            XB[o, s].wait_recv()
-            XH[o, s] = gsend(chunk(xx(-s), zz(o), cols_b, half_of(s)), xdev(s))
-
-    def finish_xh(o):
-        for s in SIGNS:
-            XH[o, s].wait_recv()
-
-    def forward_zb(d):
-        for s in SIGNS:
-            ZB[d, s].wait_recv()
-            if d < 3:
-                ZB[d + 1, s] = gsend(chunk(x, zz(-s * d), cols_b), zdev(s))
-            elif d == 3:
-                ZB[d + 1, s] = gsend(chunk(x, zz(-s * d), cols_b, half_of(s)), zdev(s))
-
-    def forward_za(d):
-        for cp in range(2):
-            for s in SIGNS:
-                if (d, s, cp) not in ZA:
-                    continue
-                ZA[d, s, cp].wait_recv()
-                if d < 3 or (d == 3 and cp == (0 if s > 0 else 1)):
-                    ZA[d + 1, s, cp] = gsend(plane(cp, zz(-s * d)), zdev(s))
+
+    def chunk(dx, dz, first, last, side=0):
+        xp, zp = xx(dx), zz(dz)
+        rows = {0: pl.ds(0, rows_dev), 1: pl.ds(0, half), -1: pl.ds(half, half)}[side]
+        return G.at[xp // 2, zp, xp % 2, rows, pl.ds(first, last - first)]
+
+    def own_column(o):
+        if o == 0:
+            return []
+        return [(ZB, 4, 1), (ZB, 4, -1)] if o == 4 else [(ZB, abs(o), -1 if o > 0 else 1)]
+
+    def message(kind, *at):
+        if kind == XA1:
+            (s,) = at
+            return chunk(0, 0, 0, CUT_OWN), xdev(s), []
+        if kind == XA2:
+            (s,) = at
+            return chunk(-s, 0, 0, CUT_OWN, s), xdev(s), [(XA1, s)]
+        if kind == ZB:
+            d, s = at
+            side = s if d == 4 else 0
+            return chunk(0, -s * (d - 1), CUT_NEXT, columns, side), zdev(s), [(ZB, d - 1, s)] if d > 1 else []
+        if kind == XB:
+            o, s = at
+            return chunk(0, o, CUT_NEXT if o else CUT_OWN, columns), xdev(s), own_column(o)
+        if kind == XH:
+            o, s = at
+            return chunk(-s, o, CUT_FAR if o else CUT_OWN, columns, s), xdev(s), [(XB, o, s)]
+        d, s, r = at
+        first = {0: [], 1: [(XA1, -1)], -1: [(XA1, 1)], 2: [(XA2, 1), (XA2, -1)]}[r]
+        after = [(ZA, d - 1, s, r)] if d > 1 else first
+        return chunk(r, -s * (d - 1), 0, CUT_FAR if r == 2 else CUT_NEXT), zdev(s), after
+
+    def whole(o):
+        keys = [(kind, o, s) for kind in (XB, XH) for s in (1, -1)] + own_column(o)
+        if o == 0:
+            return keys + [(kind, s) for kind in (XA1, XA2) for s in (1, -1)]
+        if o == 4:
+            return keys + [(ZA, 4, 1, 0), (ZA, 4, 1, 1), (ZA, 4, -1, 2), (ZA, 4, -1, -1)]
+        return keys + [(ZA, abs(o), -1 if o > 0 else 1, r) for r in (0, 1, -1, 2)]
+
+    sent, received = {}, set()
+
+    def receive(keys):
+        for key in keys:
+            if key not in received:
+                received.add(key)
+                sent[key].wait_recv()
 
     def product(o):
         zp = zz(o)
@@ -253,114 +275,52 @@
                     ci_copy(o, 0, Ci.at[:, zz(o)], fdev(0, 1)).wait_send()
                 ci_copy(o, 2, Ci.at[:, zz(o)], fdev(0, 1)).wait_send()
 
-    for s in SIGNS:
-        XA1[s] = gsend(chunk(x, z, cols_a), xdev(s))
-    for s in SIGNS:
-        ZB[1, s] = gsend(chunk(x, z, cols_b), zdev(s))
-    start_xb(0)
-    for s in SIGNS:
-        XA1[s].wait_recv()
-        XA2[s] = gsend(chunk(xx(-s), z, cols_a, half_of(s)), xdev(s))
-    forward_zb(1)
-    start_xb(1)
-    start_xb(-1)
-    forward_xb(0)
-    for s in SIGNS:
-        XA2[s].wait_recv()
-    for cp in range(2):
-        for s in SIGNS:
-            ZA[1, s, cp] = gsend(plane(cp, z), zdev(s))
-    WX = [remote(wt, wx.at[d], ws.at[d - 1], wr.at[d - 1], xdev(d)) for d in range(1, NX)]
-    fcopy.wait()
-
-    forward_zb(2)
-    start_xb(2)
-    start_xb(-2)
-    forward_xb(1)
-    forward_xb(-1)
-    finish_xh(0)
-    ci_root(0)
-    product(0)
-    send_half(0)
-    forward_zb(3)
-    start_xb(3)
-    start_xb(-3)
-    forward_za(1)
-    send_quarters(0)
-    finish_xh(1)
-    finish_xh(-1)
-    ci_root(1)
-    ci_root(-1)
-    product(1)
-    send_half(1)
-    product(-1)
-    send_half(-1)
-    ci_near(0)
-    forward_xb(2)
-    forward_xb(-2)
-    forward_zb(4)
-    start_xb(4)
-    total = wt[...]
-    for d in range(1, NX):
-        WX[d - 1].wait_recv()
-        total = total + wx[d]
-    wz0[...] = total
-    WZ = [remote(wz0, wz.at[d], ws.at[d + 2], wr.at[d + 2], zdev(d)) for d in range(1, NZ)]
-    squares(0)
-    send_quarters(1)
-    send_quarters(-1)
-    forward_za(2)
-    finish_xh(2)
-    finish_xh(-2)
-    ci_root(2)
-    ci_root(-2)
-    product(2)
-    send_half(2)
-    product(-2)
-    send_half(-2)
-    ci_far(0)
-    ci_near(1)
-    ci_near(-1)
-    forward_xb(3)
-    forward_xb(-3)
-    squares(1)
-    squares(-1)
-    send_quarters(2)
-    send_quarters(-2)
-    forward_za(3)
-    finish_xh(3)
-    finish_xh(-3)
-    ci_root(3)
-    ci_root(-3)
-    product(3)
-    send_half(3)
-    product(-3)
-    send_half(-3)
-    forward_xb(4)
-    squares(2)
-    squares(-2)
-    send_quarters(3)
-    send_quarters(-3)
-    ci_far(1)
-    ci_far(-1)
-    ci_near(2)
-    ci_near(-2)
-    forward_za(4)
-    total = wz0[...]
-    for d in range(1, NZ):
-        WZ[d - 1].wait_recv()
-        total = total + wz[d]
-    wz0_all = total
-    finish_xh(4)
-    product(4)
-    send_half(4)
-    send_quarters(4)
-    ci_root(4)
-    squares(3)
-    squares(-3)
-    for o in (0, 1, -1):
-        ci_last(o)
-    squares(4)
+    WX, WZ = [], []
+    near, far = [], []
+    for op in ORDER:
+        kind, at = op[0], op[1:]
+        if kind <= ZA:
+            view, dev, after = message(*op)
+            receive(after)
+            sent[op] = gsend(view, dev)
+        elif kind == PRODUCT:
+            (o,) = at
+            receive(whole(o))
+            if o == 0:
+                fcopy.wait()
+            if o != 4:
+                ci_root(o)
+            product(o)
+            send_half(o)
+            if o == 0:
+                WX = [remote(wt, wx.at[d], ws.at[d - 1], wr.at[d - 1], xdev(d)) for d in range(1, NX)]
+            if o == -2:
+                total = wt[...]
+                for d in range(1, NX):
+                    WX[d - 1].wait_recv()
+                    total = total + wx[d]
+                wz0[...] = total
+                receive(own_column(4))
+                WZ = [remote(wz0, wz.at[d], ws.at[d + 2], wr.at[d + 2], zdev(d)) for d in range(1, NZ)]
+        elif kind == QUARTERS:
+            send_quarters(*at)
+            if at == (4,):
+                ci_root(4)
+                for o in OFFSETS[:-1]:
+                    if o not in near:
+                        ci_near(o)
+                        near.append(o)
+                last = list(far)
+                for o in last:
+                    ci_last(o)
+        elif kind == SQUARES:
+            squares(*at)
+        elif kind == NEAR:
+            ci_near(*at)
+            near += at
+        else:
+            ci_far(*at)
+            far += at
 
     lz0[...] = V[...]
     for k, (dx, dz) in enumerate(plane_peers):
@@ -368,13 +328,16 @@
     all_sums = pltpu.make_async_remote_copy(
         src_ref=lz, dst_ref=lz, send_sem=ls.at[0], recv_sem=lr.at[0], device_id=xdev(1), device_id_type=MESH
     )
-    for o in (2, -2):
-        ci_far(o)
-    for o in (3, -3):
-        ci_near(o)
     ci_near(4)
-    for o in (2, -2):
-        ci_last(o)
+    for o in OFFSETS[:-1]:
+        if o not in far:
+            ci_far(o)
+            far.append(o)
+    total = wz0[...]
+    for d in range(1, NZ):
+        WZ[d - 1].wait_recv()
+        total = total + wz[d]
+    wz0_all = total
     v = lz0[...]
     all_sums.wait_recv()
     for k in range(len(plane_peers)):
@@ -396,10 +359,12 @@
 
     mass = over_strata(weights)
     all_sums.wait_send()
-    for o in (3, -3, 4):
-        ci_far(o)
-    for o in (3, -3, 4):
-        ci_last(o)
+    for o in OFFSETS:
+        if o not in far:
+            ci_far(o)
+    for o in OFFSETS:
+        if o not in last:
+            ci_last(o)
     for cp in pending:
         cp.wait_send()
     for o in OFFSETS:
@@ -475,8 +440,8 @@
             pltpu.VMEM((NZ, 128), f32),
             pltpu.VMEM((NZ, NZ, 128), f32),
             dma((4,)),
-            dma((58,)),
-            dma((58,)),
+            dma((72,)),
+            dma((72,)),
             dma((10,)),
             dma((10,)),
             dma((8,)),

time: 89.1 us -> 86.5 us (0.971)
  Pallas kernels: 88.2 us -> 85.8 us
    pallas_call x1, Pallas kernels: 82.7 us -> 80.3 us  [gather(): pl.pallas_call(gather_kernel, out_shape=(pltpu.VMEM((2, NZ, 2, rows_dev,...]
where the time goes in v4:
time: 86.5 us; the launch traced here: 86.4 us
  Pallas kernels  85.8 us (99%)
    pallas_call x1, Pallas kernels, gather(): pl.pallas_call(gather_kernel, out_shape=(pltpu.VMEM((2, NZ, 2, rows_dev,...  80.3 us
    pallas_call x1, Pallas kernels, increment(): pl.pallas_call(increment_kernel, out_shape=(pltpu.HBM((rows, columns), f3...  5.52 us

profile of v4, /device:TPU:1, one launch (start us, length us, event | category | flops | bytes accessed | tf_op | source)
XLA Modules:
  0.0 86.4 jit_solution(3255047829154184742)
XLA Ops:
  0.6 80.3 %shard_map.67 = (bf16[2,8,2,64,2048]{4,3,2,1,0:T(8,128)(2,1)S(1)}, bf16[512,2048]{1,0:T(8,128)(2,1)S(1)}, f32[1,64]{1,0:T(1,128)S(1)}, f32[1,64]{1,0:T(1,128)S(1)}) custom-call(bf16[64,2048]{1,0:T(8,128)(2,1)} %cand.1, bf16[512,2048]{1,0:T(8,128)(2,1)} %fac.1, f32[1,64]{1,0:T(1,128)} %bitcast.6, s32[1,64]{1,0:T(1,128)} %bitcast.7), custom_call_target="tpu_custom_call" | custom-call | tf_op jit(solution)/shard_map/pallas_call | solution.py:413
  80.9 5.5 %shard_map.68 = (f32[512,2048]{1,0:T(8,128)}, f32[1,64]{1,0:T(1,128)}, f32[1,64]{1,0:T(1,128)}) custom-call(bf16[512,2048]{1,0:T(8,128)(2,1)S(1)} %get-tuple-element.10.s_ref, bf16[2048,2048]{1,0:T(8,128)(2,1)S(1)} %bitcast.5, f32[1,64]{1,0:T(1,128)S(1)} %get-tuple-element.12.nw_ref, f32[1,64]{1,0:T(1,128)S(1)} %get-tuple-element.13.lev_ref), custom_call_target="tpu_custom_call" | custom-call | tf_op jit(solution)/shard_map/pallas_call | solution.py:491

commit v5 on v4

--- a/solution.py
+++ b/solution.py
@@ -15,19 +15,19 @@
 XA1, XA2, ZB, XB, XH, ZA, PRODUCT, QUARTERS, SQUARES, NEAR, FAR = range(11)
 ORDER = (
     (ZB, 1, -1), (ZB, 1, 1), (XA1, -1), (XA1, 1), (XB, 0, -1), (XB, 0, 1), (ZA, 1, -1, 0), (ZA, 1, 1, 0),
-    (XA2, -1), (ZA, 1, -1, 1), (XA2, 1), (ZA, 1, 1, 1), (ZA, 1, -1, -1), (ZA, 1, 1, -1), (XB, 1, -1),
-    (XB, 1, 1), (ZB, 2, -1), (ZB, 2, 1), (XB, -1, -1), (XB, -1, 1), (ZA, 1, -1, 2), (ZA, 1, 1, 2),
-    (XH, 0, -1), (XH, 0, 1), (ZA, 2, -1, 0), (ZA, 2, 1, 0), (XH, 1, -1), (XH, 1, 1), (ZA, 2, -1, 1),
-    (ZA, 2, 1, 1), (XB, 2, -1), (XB, 2, 1), (ZB, 3, -1), (ZB, 3, 1), (XH, -1, -1), (XH, -1, 1), (PRODUCT, 0),
-    (XB, -2, -1), (XB, -2, 1), (PRODUCT, 1), (ZA, 2, -1, -1), (ZA, 2, 1, -1), (QUARTERS, 0), (QUARTERS, 1),
-    (ZA, 2, -1, 2), (ZA, 2, 1, 2), (XH, 2, -1), (XH, 2, 1), (SQUARES, 0), (PRODUCT, -1), (ZA, 3, -1, 0),
-    (ZA, 3, 1, 0), (SQUARES, 1), (XB, 3, -1), (XB, 3, 1), (QUARTERS, -1), (NEAR, 0), (ZB, 4, -1), (ZB, 4, 1),
-    (XB, -3, -1), (XB, -3, 1), (NEAR, 1), (ZA, 3, -1, 1), (ZA, 3, 1, 1), (SQUARES, -1), (PRODUCT, 2),
-    (ZA, 3, -1, -1), (ZA, 3, 1, -1), (XH, -2, -1), (XH, -2, 1), (QUARTERS, 2), (ZA, 3, -1, 2), (ZA, 3, 1, 2),
-    (NEAR, -1), (XH, 3, -1), (XH, 3, 1), (XB, 4, -1), (XB, 4, 1), (ZA, 4, 1, 0), (SQUARES, 2), (FAR, 0),
-    (ZA, 4, 1, 1), (FAR, 1), (XH, -3, -1), (XH, -3, 1), (PRODUCT, -2), (ZA, 4, -1, -1), (NEAR, 2),
-    (QUARTERS, -2), (ZA, 4, -1, 2), (PRODUCT, 3), (FAR, -1), (QUARTERS, 3), (XH, 4, -1), (XH, 4, 1),
-    (SQUARES, -2), (PRODUCT, -3), (SQUARES, 3), (QUARTERS, -3), (PRODUCT, 4), (QUARTERS, 4), (SQUARES, -3),
+    (XA2, -1), (ZA, 1, -1, 1), (XA2, 1), (ZA, 1, 1, 1), (XB, 1, -1), (XB, 1, 1), (ZB, 2, -1), (ZB, 2, 1),
+    (XH, 0, -1), (XH, 0, 1), (ZA, 1, -1, -1), (ZA, 1, 1, -1), (XB, -1, -1), (XB, -1, 1), (ZA, 1, -1, 2),
+    (ZA, 1, 1, 2), (XH, 1, -1), (XH, 1, 1), (ZB, 3, -1), (ZB, 3, 1), (PRODUCT, 0), (XB, 2, -1), (XB, 2, 1),
+    (QUARTERS, 0), (ZA, 2, -1, 0), (ZA, 2, 1, 0), (XH, -1, -1), (XH, -1, 1), (PRODUCT, 1), (ZA, 2, -1, 1),
+    (ZA, 2, 1, 1), (XB, -2, -1), (XB, -2, 1), (SQUARES, 0), (QUARTERS, 1), (ZB, 4, -1), (ZB, 4, 1), (NEAR, 0),
+    (ZA, 2, -1, -1), (ZA, 2, 1, -1), (XH, 2, -1), (XH, 2, 1), (PRODUCT, -1), (ZA, 2, -1, 2), (ZA, 2, 1, 2),
+    (XB, 3, -1), (XB, 3, 1), (SQUARES, 1), (QUARTERS, -1), (NEAR, 1), (ZA, 3, -1, 0), (ZA, 3, 1, 0),
+    (XH, -2, -1), (XH, -2, 1), (SQUARES, -1), (ZA, 3, -1, 1), (ZA, 3, 1, 1), (XB, -3, -1), (XB, -3, 1),
+    (PRODUCT, 2), (ZA, 3, -1, -1), (ZA, 3, 1, -1), (FAR, 0), (NEAR, -1), (QUARTERS, 2), (XH, 3, -1),
+    (XH, 3, 1), (ZA, 3, -1, 2), (ZA, 3, 1, 2), (PRODUCT, -2), (XB, 4, -1), (XB, 4, 1), (QUARTERS, -2),
+    (ZA, 4, 1, 0), (FAR, 1), (SQUARES, 2), (ZA, 4, -1, -1), (ZA, 4, 1, 1), (XH, -3, -1), (XH, -3, 1),
+    (SQUARES, -2), (NEAR, 2), (ZA, 4, -1, 2), (PRODUCT, 3), (QUARTERS, 3), (FAR, -1), (NEAR, -2), (XH, 4, -1),
+    (XH, 4, 1), (PRODUCT, -3), (SQUARES, 3), (QUARTERS, -3), (PRODUCT, 4), (QUARTERS, 4), (SQUARES, -3),
     (SQUARES, 4),
 )
 
@@ -56,7 +56,7 @@
         ((dx, dz) for dx in range(NX) for dz in range(NZ) if (dx, dz) != (0, 0)),
         key=lambda d: -(min(d[0], NX - d[0]) + min(d[1], NZ - d[1])),
     )
-    fcopies = [(dy, dc) for dy in range(NY) for dc in range(NC) if (dy, dc) != (0, 0)]
+    fcopies = [(dy, dc) for dy in (2, 1, 3, 0) for dc in range(NC) if (dy, dc) != (0, 0)]
 
     def xx(d):
         return lax.rem(x + d + NX, NX)
@@ -190,7 +190,7 @@
         PX[o].wait_recv()
         q = pb[zp, c].astype(jnp.float32) + px[zp].astype(jnp.float32)
         ysb[zp] = q.astype(jnp.bfloat16).reshape(NY, 128, 128)
-        for d in range(1, NY):
+        for d in (2, 1, 3):
             yp = lax.rem(y + d, NY)
             YS[o, d] = remote(
                 ysb.at[zp, yp], ysr.at[zp, d], yss.at[i * 3 + d - 1], ysrs.at[i * 3 + d - 1], fdev(d, 0)

time: 86.5 us -> 84.1 us (0.972)
  Pallas kernels: 85.8 us -> 83.4 us
    pallas_call x1, Pallas kernels: 80.3 us -> 77.8 us  [gather(): pl.pallas_call(gather_kernel, out_shape=(pltpu.VMEM((2, NZ, 2, rows_dev,...]
where the time goes in v5:
time: 84.1 us; the launch traced here: 84 us
  Pallas kernels  83.4 us (99%)
    pallas_call x1, Pallas kernels, gather(): pl.pallas_call(gather_kernel, out_shape=(pltpu.VMEM((2, NZ, 2, rows_dev,...  77.8 us
    pallas_call x1, Pallas kernels, increment(): pl.pallas_call(increment_kernel, out_shape=(pltpu.HBM((rows, columns), f3...  5.52 us

profile of v5, /device:TPU:1, one launch (start us, length us, event | category | flops | bytes accessed | tf_op | source)
XLA Modules:
  0.0 84.0 jit_solution(2534637303009862520)
XLA Ops:
  0.6 77.8 %shard_map.67 = (bf16[2,8,2,64,2048]{4,3,2,1,0:T(8,128)(2,1)S(1)}, bf16[512,2048]{1,0:T(8,128)(2,1)S(1)}, f32[1,64]{1,0:T(1,128)S(1)}, f32[1,64]{1,0:T(1,128)S(1)}) custom-call(bf16[64,2048]{1,0:T(8,128)(2,1)} %cand.1, bf16[512,2048]{1,0:T(8,128)(2,1)} %fac.1, f32[1,64]{1,0:T(1,128)} %bitcast.6, s32[1,64]{1,0:T(1,128)} %bitcast.7), custom_call_target="tpu_custom_call" | custom-call | tf_op jit(solution)/shard_map/pallas_call | solution.py:413
  78.5 5.5 %shard_map.68 = (f32[512,2048]{1,0:T(8,128)}, f32[1,64]{1,0:T(1,128)}, f32[1,64]{1,0:T(1,128)}) custom-call(bf16[512,2048]{1,0:T(8,128)(2,1)S(1)} %get-tuple-element.10.s_ref, bf16[2048,2048]{1,0:T(8,128)(2,1)S(1)} %bitcast.5, f32[1,64]{1,0:T(1,128)S(1)} %get-tuple-element.12.nw_ref, f32[1,64]{1,0:T(1,128)S(1)} %get-tuple-element.13.lev_ref), custom_call_target="tpu_custom_call" | custom-call | tf_op jit(solution)/shard_map/pallas_call | solution.py:491

commit v6 on v5

--- a/solution.py
+++ b/solution.py
@@ -337,36 +337,36 @@
     for d in range(1, NZ):
         WZ[d - 1].wait_recv()
         total = total + wz[d]
-    wz0_all = total
+    weights, labels = [total[0], total[1]], [total[2], total[3]]
+    ids = lax.broadcasted_iota(jnp.int32, (STRATA, 128), 0).astype(jnp.float32)
+
+    def over_strata(tiles):
+        acc = jnp.zeros((STRATA, 128), jnp.float32)
+        for cp in range(2):
+            for zp in range(NZ):
+                acc = acc + jnp.where(labels[cp][zp : zp + 1, :] == ids, tiles[cp][zp : zp + 1, :], 0.0)
+        return jnp.sum(acc, axis=1, keepdims=True)
+
+    mass = over_strata(weights)
+    for cp in pending:
+        cp.wait_send()
+    late = OFFSETS[-3:]
+    for o in OFFSETS:
+        if o not in last and o not in late:
+            ci_last(o)
     v = lz0[...]
     all_sums.wait_recv()
     for k in range(len(plane_peers)):
         v = v + lz[k]
     lt0[...] = v
     LT = [
-        remote(lt0, lt.at[k], ls.at[k + 9], lr.at[k + 9], fdev(*d)) for k, d in enumerate(fcopies, 1)
+        remote(lt0, lt.at[k], ls.at[k + 9], lr.at[k + 9], fdev(*d), keep=False)
+        for k, d in enumerate(fcopies, 1)
     ]
-    weights = [wz0_all[0], wz0_all[1]]
-    labels = [wz0_all[2], wz0_all[3]]
-    ids = lax.broadcasted_iota(jnp.int32, (STRATA, 128), 0).astype(jnp.float32)
-
-    def over_strata(tiles):
-        acc = jnp.zeros((STRATA, 128), jnp.float32)
-        for cp in range(2):
-            for zp in range(NZ):
-                acc = acc + jnp.where(labels[cp][zp : zp + 1, :] == ids, tiles[cp][zp : zp + 1, :], 0.0)
-        return jnp.sum(acc, axis=1, keepdims=True)
-
-    mass = over_strata(weights)
     all_sums.wait_send()
-    for o in OFFSETS:
-        if o not in far:
-            ci_far(o)
-    for o in OFFSETS:
-        if o not in last:
-            ci_last(o)
-    for cp in pending:
-        cp.wait_send()
+    ci_far(4)
+    for o in late:
+        ci_last(o)
     for o in OFFSETS:
         ci_finish(o)
     same, other = lt0[...], None
@@ -401,6 +401,8 @@
 
     nw_ref[...] = own_rows(new_weights)
     lev_ref[...] = own_rows(raw) / features
+    for cp in LT:
+        cp.wait_send()
 
 
 def gather(cand, fac, weights, strata):

time: 84.1 us -> 84.1 us (level)
  no operation moved by 1% of the time
where the time goes in v6:
time: 84.1 us; the launch traced here: 84 us
  Pallas kernels  83.3 us (99%)
    pallas_call x1, Pallas kernels, gather(): pl.pallas_call(gather_kernel, out_shape=(pltpu.VMEM((2, NZ, 2, rows_dev,...  77.8 us
    pallas_call x1, Pallas kernels, increment(): pl.pallas_call(increment_kernel, out_shape=(pltpu.HBM((rows, columns), f3...  5.52 us

profile of v6, /device:TPU:1, one launch (start us, length us, event | category | flops | bytes accessed | tf_op | source)
XLA Modules:
  0.0 84.0 jit_solution(11257942752337804483)
XLA Ops:
  0.6 77.8 %shard_map.67 = (bf16[2,8,2,64,2048]{4,3,2,1,0:T(8,128)(2,1)S(1)}, bf16[512,2048]{1,0:T(8,128)(2,1)S(1)}, f32[1,64]{1,0:T(1,128)S(1)}, f32[1,64]{1,0:T(1,128)S(1)}) custom-call(bf16[64,2048]{1,0:T(8,128)(2,1)} %cand.1, bf16[512,2048]{1,0:T(8,128)(2,1)} %fac.1, f32[1,64]{1,0:T(1,128)} %bitcast.6, s32[1,64]{1,0:T(1,128)} %bitcast.7), custom_call_target="tpu_custom_call" | custom-call | tf_op jit(solution)/shard_map/pallas_call | solution.py:415
  78.5 5.5 %shard_map.68 = (f32[512,2048]{1,0:T(8,128)}, f32[1,64]{1,0:T(1,128)}, f32[1,64]{1,0:T(1,128)}) custom-call(bf16[512,2048]{1,0:T(8,128)(2,1)S(1)} %get-tuple-element.10.s_ref, bf16[2048,2048]{1,0:T(8,128)(2,1)S(1)} %bitcast.5, f32[1,64]{1,0:T(1,128)S(1)} %get-tuple-element.12.nw_ref, f32[1,64]{1,0:T(1,128)S(1)} %get-tuple-element.13.lev_ref), custom_call_target="tpu_custom_call" | custom-call | tf_op jit(solution)/shard_map/pallas_call | solution.py:493

commit v7 on v6

--- a/solution.py
+++ b/solution.py
@@ -15,20 +15,20 @@
 XA1, XA2, ZB, XB, XH, ZA, PRODUCT, QUARTERS, SQUARES, NEAR, FAR = range(11)
 ORDER = (
     (ZB, 1, -1), (ZB, 1, 1), (XA1, -1), (XA1, 1), (XB, 0, -1), (XB, 0, 1), (ZA, 1, -1, 0), (ZA, 1, 1, 0),
-    (XA2, -1), (ZA, 1, -1, 1), (XA2, 1), (ZA, 1, 1, 1), (XB, 1, -1), (XB, 1, 1), (ZB, 2, -1), (ZB, 2, 1),
-    (XH, 0, -1), (XH, 0, 1), (ZA, 1, -1, -1), (ZA, 1, 1, -1), (XB, -1, -1), (XB, -1, 1), (ZA, 1, -1, 2),
-    (ZA, 1, 1, 2), (XH, 1, -1), (XH, 1, 1), (ZB, 3, -1), (ZB, 3, 1), (PRODUCT, 0), (XB, 2, -1), (XB, 2, 1),
-    (QUARTERS, 0), (ZA, 2, -1, 0), (ZA, 2, 1, 0), (XH, -1, -1), (XH, -1, 1), (PRODUCT, 1), (ZA, 2, -1, 1),
-    (ZA, 2, 1, 1), (XB, -2, -1), (XB, -2, 1), (SQUARES, 0), (QUARTERS, 1), (ZB, 4, -1), (ZB, 4, 1), (NEAR, 0),
-    (ZA, 2, -1, -1), (ZA, 2, 1, -1), (XH, 2, -1), (XH, 2, 1), (PRODUCT, -1), (ZA, 2, -1, 2), (ZA, 2, 1, 2),
-    (XB, 3, -1), (XB, 3, 1), (SQUARES, 1), (QUARTERS, -1), (NEAR, 1), (ZA, 3, -1, 0), (ZA, 3, 1, 0),
-    (XH, -2, -1), (XH, -2, 1), (SQUARES, -1), (ZA, 3, -1, 1), (ZA, 3, 1, 1), (XB, -3, -1), (XB, -3, 1),
-    (PRODUCT, 2), (ZA, 3, -1, -1), (ZA, 3, 1, -1), (FAR, 0), (NEAR, -1), (QUARTERS, 2), (XH, 3, -1),
-    (XH, 3, 1), (ZA, 3, -1, 2), (ZA, 3, 1, 2), (PRODUCT, -2), (XB, 4, -1), (XB, 4, 1), (QUARTERS, -2),
-    (ZA, 4, 1, 0), (FAR, 1), (SQUARES, 2), (ZA, 4, -1, -1), (ZA, 4, 1, 1), (XH, -3, -1), (XH, -3, 1),
-    (SQUARES, -2), (NEAR, 2), (ZA, 4, -1, 2), (PRODUCT, 3), (QUARTERS, 3), (FAR, -1), (NEAR, -2), (XH, 4, -1),
-    (XH, 4, 1), (PRODUCT, -3), (SQUARES, 3), (QUARTERS, -3), (PRODUCT, 4), (QUARTERS, 4), (SQUARES, -3),
-    (SQUARES, 4),
+    (XA2, -1), (ZA, 1, -1, 1), (XA2, 1), (ZA, 1, 1, 1), (ZA, 1, -1, -1), (ZA, 1, 1, -1), (XB, 1, -1),
+    (XB, 1, 1), (ZB, 2, -1), (ZB, 2, 1), (XH, 0, -1), (XH, 0, 1), (XB, -1, -1), (XB, -1, 1), (ZA, 1, -1, 2),
+    (ZA, 1, 1, 2), (XH, 1, -1), (XH, 1, 1), (ZA, 2, -1, 0), (ZA, 2, 1, 0), (PRODUCT, 0), (XB, 2, -1),
+    (XB, 2, 1), (ZB, 3, -1), (ZB, 3, 1), (QUARTERS, 0), (XH, -1, -1), (XH, -1, 1), (ZA, 2, -1, 1),
+    (ZA, 2, 1, 1), (PRODUCT, 1), (XB, -2, -1), (XB, -2, 1), (SQUARES, 0), (QUARTERS, 1), (ZA, 2, -1, -1),
+    (ZA, 2, 1, -1), (NEAR, 0), (ZA, 2, -1, 2), (ZA, 2, 1, 2), (XH, 2, -1), (XH, 2, 1), (PRODUCT, -1),
+    (XB, 3, -1), (XB, 3, 1), (SQUARES, 1), (ZB, 4, -1), (ZB, 4, 1), (QUARTERS, -1), (ZA, 3, -1, 0),
+    (ZA, 3, 1, 0), (NEAR, 1), (XH, -2, -1), (XH, -2, 1), (SQUARES, -1), (ZA, 3, -1, 1), (ZA, 3, 1, 1),
+    (PRODUCT, 2), (XB, -3, -1), (XB, -3, 1), (ZA, 3, -1, -1), (ZA, 3, 1, -1), (FAR, 0), (QUARTERS, 2),
+    (NEAR, -1), (XH, 3, -1), (XH, 3, 1), (ZA, 3, -1, 2), (ZA, 3, 1, 2), (PRODUCT, -2), (XB, 4, -1),
+    (XB, 4, 1), (SQUARES, 2), (QUARTERS, -2), (ZA, 4, 1, 0), (FAR, 1), (ZA, 4, -1, -1), (ZA, 4, 1, 1),
+    (NEAR, 2), (XH, -3, -1), (XH, -3, 1), (SQUARES, -2), (ZA, 4, -1, 2), (PRODUCT, 3), (FAR, -1),
+    (QUARTERS, 3), (NEAR, -2), (XH, 4, -1), (XH, 4, 1), (PRODUCT, -3), (SQUARES, 3), (QUARTERS, -3),
+    (PRODUCT, 4), (QUARTERS, 4), (SQUARES, -3), (SQUARES, 4),
 )
 
 

time: 84.1 us -> 84 us (level)
  no operation moved by 1% of the time
where the time goes in v7:
time: 84 us; the launch traced here: 83.9 us
  Pallas kernels  83.3 us (99%)
    pallas_call x1, Pallas kernels, gather(): pl.pallas_call(gather_kernel, out_shape=(pltpu.VMEM((2, NZ, 2, rows_dev,...  77.8 us
    pallas_call x1, Pallas kernels, increment(): pl.pallas_call(increment_kernel, out_shape=(pltpu.HBM((rows, columns), f3...  5.52 us

profile of v7, /device:TPU:1, one launch (start us, length us, event | category | flops | bytes accessed | tf_op | source)
XLA Modules:
  0.0 83.9 jit_solution(43261612150991842)
XLA Ops:
  0.6 77.8 %shard_map.67 = (bf16[2,8,2,64,2048]{4,3,2,1,0:T(8,128)(2,1)S(1)}, bf16[512,2048]{1,0:T(8,128)(2,1)S(1)}, f32[1,64]{1,0:T(1,128)S(1)}, f32[1,64]{1,0:T(1,128)S(1)}) custom-call(bf16[64,2048]{1,0:T(8,128)(2,1)} %cand.1, bf16[512,2048]{1,0:T(8,128)(2,1)} %fac.1, f32[1,64]{1,0:T(1,128)} %bitcast.6, s32[1,64]{1,0:T(1,128)} %bitcast.7), custom_call_target="tpu_custom_call" | custom-call | tf_op jit(solution)/shard_map/pallas_call | solution.py:415
  78.4 5.5 %shard_map.68 = (f32[512,2048]{1,0:T(8,128)}, f32[1,64]{1,0:T(1,128)}, f32[1,64]{1,0:T(1,128)}) custom-call(bf16[512,2048]{1,0:T(8,128)(2,1)S(1)} %get-tuple-element.10.s_ref, bf16[2048,2048]{1,0:T(8,128)(2,1)S(1)} %bitcast.5, f32[1,64]{1,0:T(1,128)S(1)} %get-tuple-element.12.nw_ref, f32[1,64]{1,0:T(1,128)S(1)} %get-tuple-element.13.lev_ref), custom_call_target="tpu_custom_call" | custom-call | tf_op jit(solution)/shard_map/pallas_call | solution.py:493
